TPU v7x, 32 devices: a whole 2x2x4 slice. The times are simulated.
32 devices in a mesh: kind: 2 (over core), dp: 8 (over z, x), inner: 2 (over y).
Axes of the slice: x: 2, y: 2, z: 4, core: 2. Of those that a mesh axis runs over, the one named last changes fastest.
Arguments:
- layer_input: bfloat16 [16, 1024, 512], P('dp', 'inner'), may hold values from -6 to 6
- output_grad: bfloat16 [16, 1024, 512], P('dp'), may hold values from -6 to 6
- document_ids: int32 [16, 1024], P('dp'), may hold values from 0 to 8, as said below
- mamba_gain: float32 [512], replicated, may hold values from 0.1 to 1.9
- in_proj: bfloat16 [512, 2048], replicated, may hold values from -0.25 to 0.25
- conv_weight: float32 [1024, 4], replicated, may hold values from -3 to 3
- conv_bias: float32 [1024], replicated, may hold values from -0.5 to 0.5
- state_proj: bfloat16 [1024, 64], replicated, may hold values from -0.1875 to 0.1875
- step_proj: bfloat16 [32, 1024], replicated, may hold values from -1 to 1
- step_bias: float32 [1024], replicated, may hold values from -7 to -2.3
- decay_log: float32 [1024, 16], replicated, may hold values from -4 to 2.5
- skip_gain: float32 [1024], replicated, may hold values from 0.5 to 1.5
- out_proj: bfloat16 [1024, 512], replicated, may hold values from -0.1875 to 0.1875
- attn_gain: float32 [512], replicated, may hold values from 0.1 to 1.9
- query_proj: bfloat16 [512, 512], replicated, may hold values from -0.25 to 0.25
- key_proj: bfloat16 [512, 512], replicated, may hold values from -0.25 to 0.25
- value_proj: bfloat16 [512, 512], replicated, may hold values from -0.25 to 0.25
- mixed_proj: bfloat16 [512, 512], replicated, may hold values from -0.75 to 0.75
Outputs:
- results: float32 [2, 16, 1024, 512], P('kind', 'dp', 'inner')
- grad_mamba_gain: float32 [512], replicated
- grad_in_proj: float32 [512, 2048], replicated
- grad_conv_weight: float32 [1024, 4], replicated
- grad_conv_bias: float32 [1024], replicated
- grad_state_proj: float32 [1024, 64], replicated
- grad_step_proj: float32 [32, 1024], replicated
- grad_step_bias: float32 [1024], replicated
- grad_decay_log: float32 [1024, 16], replicated
- grad_skip_gain: float32 [1024], replicated
- grad_out_proj: float32 [1024, 512], replicated
- grad_attn_gain: float32 [512], replicated
- grad_query: float32 [512, 512], replicated
- grad_key: float32 [512, 512], replicated
- grad_value: float32 [512, 512], replicated
- grad_mixed: float32 [512, 512], replicated
Inputs may be any that keep to these rules, and one draw needn't show every extreme that they name: `document_ids`: in each row the ids start at 0 and rise by one at each document's first token; every row holds exactly 9 documents, 4 of them starting before position 256 and 4 after position 768.
All inputs are finite; a program needn't handle non-finite values.
Results may differ from a plain program's by a relative error of at most 0.013.
Values may be sent and summed in bfloat16 or wider, within the bound.
A program may use at most 384 MiB of HBM per device.

v0:
```python
import functools

import jax
import jax.numpy as jnp
from jax import lax
from jax.experimental import pallas as pl
from jax.experimental.pallas import tpu as pltpu
from jax.sharding import PartitionSpec as P

HEAD_DIM = 64
EPS = 1e-05
NEG = -1e30
FAR = 1e30
CHUNK = 16
STRETCH = 8
ROWS_STEP = 256
QUERY_BLOCK = 256
KEY_TILE = 128
VMEM_BYTES = 58 * 1024 * 1024
F32 = jnp.float32
BF16 = jnp.bfloat16


def dot_nn(a, b):
    return lax.dot_general(a, b, (((1,), (0,)), ((), ())), preferred_element_type=F32)


def dot_nt(a, b):
    return lax.dot_general(a, b, (((1,), (1,)), ((), ())), preferred_element_type=F32)


def dot_tn(a, b):
    return lax.dot_general(a, b, (((0,), (0,)), ((), ())), preferred_element_type=F32)


def silu_slope(tensor):
    sigma = jax.nn.sigmoid(tensor)
    return sigma * (1.0 + tensor * (1.0 - sigma))


def rms_scale(tensor):
    return lax.rsqrt(jnp.mean(tensor * tensor, axis=-1, keepdims=True) + EPS)


def softplus(tensor):
    return jnp.maximum(tensor, 0.0) + jnp.log1p(jnp.exp(-jnp.abs(tensor)))


def rms_back(tensor, factor, gain_vec, gradient):
    weighted = gradient * gain_vec
    spread = jnp.mean(weighted * tensor, axis=-1, keepdims=True)
    return factor * weighted - tensor * (factor * factor * factor) * spread


def spread(ref, value):
    for c in range(ref.shape[0]):
        ref[c] = value[:, c * 128 : (c + 1) * 128]


def row_of(ref, c, row, states):
    part = ref[c, pl.ds(row, 8, stride=0), :]
    return jnp.concatenate([part] * (states // 8), axis=0)


def column_of(tile, at):
    return jnp.broadcast_to(tile[:, at : at + 1], tile.shape)


def own_token(chunk, states):
    at = lax.broadcasted_iota(jnp.int32, (chunk, chunk * states), 0)
    of = lax.broadcasted_iota(jnp.int32, (chunk, chunk * states), 1) // states
    return at == of


def state_picks(chunk, states):
    at = lax.broadcasted_iota(jnp.int32, (states, chunk * states), 0)
    of = lax.rem(lax.broadcasted_iota(jnp.int32, (states, chunk * states), 1), states)
    return (at == of).astype(F32).astype(BF16)


def remote(src, dst, sems, number, to):
    return pltpu.make_async_remote_copy(
        src_ref=src, dst_ref=dst, send_sem=sems[0].at[number], recv_sem=sems[1].at[number],
        device_id=to, device_id_type=pl.DeviceIdType.MESH,
    )


def call(body, sel, steps, ins, outs, scratch, flops, name):
    bytes_all = sum(a.size * a.dtype.itemsize for a, _, _ in ins)
    return pl.pallas_call(
        body,
        grid_spec=pltpu.PrefetchScalarGridSpec(
            num_scalar_prefetch=1,
            grid=(steps,),
            in_specs=[pl.BlockSpec(block, at) for _, block, at in ins],
            out_specs=[pl.BlockSpec(block, at) for _, _, block, at in outs],
            scratch_shapes=scratch,
        ),
        out_shape=[jax.ShapeDtypeStruct(shape, dtype) for shape, dtype, _, _ in outs],
        compiler_params=pltpu.CompilerParams(
            dimension_semantics=("arbitrary",), vmem_limit_bytes=VMEM_BYTES
        ),
        cost_estimate=pl.CostEstimate(flops=flops, bytes_accessed=bytes_all, transcendentals=0),
        name=name,
    )(sel, *[a for a, _, _ in ins])


def whole(shape):
    zeros = (0,) * len(shape)
    return (shape, lambda i, sel: zeros)


def scan_block(
    coef, pre, gate, flags, step_w, step_b, decay_t, skip, out_w,
    step_o, scan_o, gated_o, starts_o, branch_o, spare,
):
    state, stepd, drive, ys, blocked, h_low = spare
    block, width = pre.shape
    states = decay_t.shape[0]
    rank = step_w.shape[0]
    tiles = width // 128

    step_pre = dot_tn(coef[:rank, :].astype(BF16), step_w[...]) + step_b[...]
    step_o[...] = step_pre
    step = softplus(step_pre)
    act = pre[...] * jax.nn.sigmoid(pre[...])
    spread(drive, step * act)
    spread(stepd, jnp.where(flags[:, 1:2] > 0.0, step, FAR))
    neg = -jnp.exp(decay_t[...])
    neg_of = [neg[:, c * 128 : (c + 1) * 128] for c in range(tiles)]
    own_all = jnp.concatenate([own_token(CHUNK, states)] * (block // CHUNK), axis=0)
    blocked[...] = jnp.where(
        own_all, dot_tn(coef[rank + states :, :].astype(BF16), state_picks(CHUNK, states)), 0.0
    ).astype(BF16)

    def one_chunk(i, h, h_s):
        here = pl.ds(pl.multiple_of(i * CHUNK, CHUNK), CHUNK)
        tile = coef[rank : rank + states, pl.ds(pl.multiple_of((i // 8) * 128, 128), 128)]
        tile = pltpu.roll(tile, lax.rem(128 - lax.rem(i, 8) * CHUNK, 128), 1)
        for c in range(tiles):
            starts_o[here, c * 128 : (c + 1) * 128] = h[c]
        for at in range(CHUNK):
            row = i * CHUNK + at
            write = column_of(tile, at)
            for c in range(tiles):
                decay = jnp.exp(neg_of[c] * row_of(stepd, c, row, states))
                h[c] = decay * h[c] + row_of(drive, c, row, states) * write
                h_s[at * states : (at + 1) * states, c * 128 : (c + 1) * 128] = h[c].astype(BF16)
        return h

    def stretch(number, carried):
        def pair(step_no, carried):
            h = list(carried)
            for sub in range(2):
                at = 2 * step_no + sub
                spot = h_low.at[pl.ds(pl.multiple_of(at * CHUNK * states, CHUNK * states), CHUNK * states)]
                h = one_chunk(number * STRETCH + at, h, spot)
            return tuple(h)

        carried = lax.fori_loop(0, STRETCH // 2, pair, carried)
        for at in range(STRETCH):
            here = pl.ds(pl.multiple_of((number * STRETCH + at) * CHUNK, CHUNK), CHUNK)
            spot = slice(at * CHUNK * states, (at + 1) * CHUNK * states)
            ys[here, :] = dot_nn(blocked[here, :], h_low[spot, :])
        return carried

    begin = tuple(state[:, c * 128 : (c + 1) * 128] for c in range(tiles))
    for c, last in enumerate(lax.fori_loop(0, block // (STRETCH * CHUNK), stretch, begin)):
        state[:, c * 128 : (c + 1) * 128] = last
    scan_out = ys[...] + skip[...] * act
    scan_o[...] = scan_out
    z = gate[...]
    gated = (scan_out * (z * jax.nn.sigmoid(z))).astype(BF16)
    gated_o[...] = gated
    branch_o[...] = dot_nn(gated, out_w[...]).astype(BF16)


def front_kernel(
    flags, gain, layer_all, weights_all,
    x_o, normed_o, conv_o, pre_o, gate_o, coef_o, step_o, scan_o, gated_o, starts_o, branch_o, branch_other_o,
    x, normed, ext, pre, gate, coef, coef_got, coef_sum, step_pre, scan_out, gated, starts, branch,
    branch_got, weights, scan_spare, load_sems, x_sems, coef_sems, branch_sems, store_sems, late_sems,
):
    length, width = x.shape
    blocks = length // ROWS_STEP
    core, row = lax.axis_index("kind"), lax.axis_index("inner")
    other_core, other_row = {"kind": 1 - core}, {"inner": 1 - row}
    w_conv, w_gate, state_w, step_w, decay_t, skip, taps, conv_b, step_b, out_w = weights
    in_all, state_all, step_all, decay_all, skip_all, taps_all, conv_b_all, step_b_all, out_all = weights_all
    channels = w_conv.shape[1]

    def part_of(number):
        return pl.ds(pl.multiple_of(number * channels, 128), channels)

    def rows_at(b):
        return pl.ds(pl.multiple_of(b * ROWS_STEP, ROWS_STEP), ROWS_STEP)

    mine = part_of(core)
    loads = [
        pltpu.make_async_copy(source, target, load_sems.at[i])
        for i, (source, target) in enumerate((
            (layer_all.at[row], x.at[pl.ds(pl.multiple_of(row * (length // 2), 256), length // 2)]),
            (in_all.at[:, mine], w_conv), (in_all.at[:, part_of(2 + core)], w_gate),
            (state_all.at[:, mine], state_w), (step_all.at[:, mine], step_w),
            (decay_all.at[:, mine], decay_t), (skip_all.at[:, mine], skip), (taps_all.at[:, mine], taps),
            (conv_b_all.at[:, mine], conv_b), (step_b_all.at[:, mine], step_b), (out_all.at[mine], out_w),
        ))
    ]
    barrier = pltpu.get_barrier_semaphore()
    for device in (other_core, other_row):
        pl.semaphore_signal(barrier, inc=1, device_id=device, device_id_type=pl.DeviceIdType.MESH)
    pl.semaphore_wait(barrier, 2)
    sent = remote(
        layer_all.at[1 - row, rows_at(core)], x.at[rows_at(row * (blocks // 2) + core)], x_sems, 0, other_row
    )
    sent.start()
    for load in loads:
        load.start()
    for load in loads:
        load.wait()
    ext[0:8, :] = jnp.zeros((8, channels), F32)
    scan_spare[0][...] = jnp.zeros_like(scan_spare[0])

    results = (
        (x, x_o), (normed, normed_o), (gate, gate_o), (pre, pre_o), (step_pre, step_o),
        (scan_out, scan_o), (gated, gated_o), (starts, starts_o), (branch, branch_o),
    )

    def stores(b, numbers=range(len(results))):
        rows = rows_at(b)
        return [
            pltpu.make_async_copy(results[i][0].at[rows], results[i][1].at[rows], store_sems.at[i, b])
            for i in numbers
        ]

    def project(b):
        rows = rows_at(b)
        u = x[rows, :].astype(F32)
        low = (u * rms_scale(u) * gain[...]).astype(BF16)
        normed[rows, :] = low
        ext[pl.ds(pl.multiple_of(b * ROWS_STEP + 8, 8), ROWS_STEP), :] = dot_nn(low, w_conv[...])
        gate[rows, :] = dot_nn(low, w_gate[...])
        for store in stores(b, range(3)):
            store.start()

    first_other = (1 - row) * (blocks // 2)
    project(row * (blocks // 2))
    project(row * (blocks // 2) + 1)
    sent.wait()
    fetched = x.at[rows_at(first_other + core)]
    passed = remote(fetched, fetched, x_sems, 1, other_core)
    passed.start()
    project(first_other + core)
    passed.wait()
    project(first_other + 1 - core)
    store_conv = pltpu.make_async_copy(ext.at[pl.ds(8, length)], conv_o, late_sems.at[0])
    store_conv.start()

    def coef_copy(b):
        return remote(coef.at[b], coef_got.at[b], coef_sems, b, other_core)

    def branch_copy(b):
        rows = rows_at(b)
        return remote(branch.at[rows], branch_got.at[rows], branch_sems, b, other_core)

    for b in range(blocks):
        rows = slice(b * ROWS_STEP, (b + 1) * ROWS_STEP)
        total = conv_b[...] + taps[3:4, :] * ext[8 + b * ROWS_STEP : 8 + (b + 1) * ROWS_STEP, :]
        for j in range(1, 4):
            moved = ext[8 - j + b * ROWS_STEP : 8 - j + (b + 1) * ROWS_STEP, :]
            total = total + taps[3 - j : 4 - j, :] * jnp.where(flags[rows, j : j + 1] > 0.0, moved, 0.0)
        pre[rows, :] = total
        coef[b] = dot_nt(state_w[...], (total * jax.nn.sigmoid(total)).astype(BF16))
        coef_copy(b).start()
        stores(b, [3])[0].start()

    def scan(b, unused):
        rows = rows_at(b)
        coef_copy(b).wait()
        coef_sum[b] = coef[b] + coef_got[b]
        scan_block(
            coef_sum.at[b], pre.at[rows], gate.at[rows], flags.at[rows], step_w, step_b, decay_t, skip, out_w,
            step_pre.at[rows], scan_out.at[rows], gated.at[rows], starts.at[rows], branch.at[rows],
            scan_spare,
        )
        branch_copy(b).start()
        for store in stores(b, range(4, len(results))):
            store.start()
        return unused

    lax.fori_loop(0, blocks, scan, 0)
    store_coef = pltpu.make_async_copy(coef_sum, coef_o, late_sems.at[1])
    store_coef.start()
    for b in range(blocks):
        branch_copy(b).wait()
    store_other = pltpu.make_async_copy(branch_got, branch_other_o, late_sems.at[2])
    store_other.start()
    for copy in (store_conv, store_coef, store_other):
        copy.wait()
    for b in range(blocks):
        for store in stores(b):
            store.wait()


def middle_kernel(
    x, part_a, part_b, first, gain, grads, gated_all, gate_all, scan_all, normed_all, weights_all,
    base_o, scan_grad_o, back_o, pack_o, gain_grad_o,
    grad, gated, gate, scan_out, normed_a, wq, wk, wv, wm, out_w, w_gate,
    normed, q_t, q_n, k_n, v_n, k_t, v_t, g_n, g_t, o_t, dq_n, dk, dv, bias, expo, prob_grad, prob_low,
    score_low,
    dq_low, dk_low, dv_low, branch, branch_got, back, back_got, base, scan_grad, gate_back, gout, ggate,
    pack, load_sems, pass_sems, store_sems,
):
    length, width = x.shape
    core, row = lax.axis_index("kind"), lax.axis_index("inner")
    other_core = {"kind": 1 - core}
    head_cols, channels = wq.shape[1], out_w.shape[0]

    def part_of(size):
        return pl.ds(pl.multiple_of(core * size, 128), size)

    query_all, key_all, value_all, mixed_all, out_all, in_all = weights_all
    gate_cols = pl.ds(pl.multiple_of((2 + core) * channels, 128), channels)
    loads = [
        pltpu.make_async_copy(source, target, load_sems.at[i])
        for i, (source, target) in enumerate((
            (query_all.at[:, part_of(head_cols)], wq), (key_all.at[:, part_of(head_cols)], wk),
            (value_all.at[:, part_of(head_cols)], wv), (grads.at[row], grad),
            (mixed_all.at[part_of(head_cols)], wm), (gated_all, gated), (gate_all, gate),
            (scan_all, scan_out), (normed_all, normed_a), (out_all.at[part_of(channels)], out_w),
            (in_all.at[:, gate_cols], w_gate),
        ))
    ]
    for load in loads:
        load.start()
    barrier = pltpu.get_barrier_semaphore()
    pl.semaphore_signal(barrier, inc=1, device_id=other_core, device_id_type=pl.DeviceIdType.MESH)
    pl.semaphore_wait(barrier, 1)
    for load in loads[:5]:
        load.wait()

    heads = k_n.shape[0]
    scale = HEAD_DIM**-0.5
    for b in range(length // ROWS_STEP):
        rows = slice(b * ROWS_STEP, (b + 1) * ROWS_STEP)
        middle = x[rows, :].astype(F32) + (part_a[rows, :].astype(F32) + part_b[rows, :].astype(F32))
        normed_blk = (middle * rms_scale(middle) * gain[...]).astype(BF16)
        normed[rows, :] = normed_blk
        query = dot_nn(normed_blk, wq[...]).astype(BF16).astype(F32) * scale
        keys = dot_nn(normed_blk, wk[...]).astype(BF16).astype(F32)
        values = dot_nn(normed_blk, wv[...]).astype(BF16).astype(F32)
        out_grad = dot_nt(grad[rows, :], wm[...]).astype(BF16).astype(F32)
        q_t[:, rows] = query.T.astype(BF16)
        k_t[:, rows] = (keys.T * scale).astype(BF16)
        v_t[:, rows] = values.T.astype(BF16)
        g_t[:, rows] = out_grad.T.astype(BF16)
        for h in range(heads):
            cols = slice(h * HEAD_DIM, (h + 1) * HEAD_DIM)
            q_n[h, rows, :] = query[:, cols].astype(BF16)
            k_n[h, rows, :] = keys[:, cols].astype(BF16)
            v_n[h, rows, :] = values[:, cols].astype(BF16)
            g_n[h, rows, :] = out_grad[:, cols].astype(BF16)
    dk[...] = jnp.zeros_like(dk)
    dv[...] = jnp.zeros_like(dv)

    for block in range(length // QUERY_BLOCK):
        cols = slice(block * QUERY_BLOCK, (block + 1) * QUERY_BLOCK)
        reach = (block + 1) * QUERY_BLOCK
        key_at = lax.broadcasted_iota(jnp.int32, (reach, QUERY_BLOCK), 0)
        query_at = lax.broadcasted_iota(jnp.int32, (reach, QUERY_BLOCK), 1) + block * QUERY_BLOCK
        kept = (key_at >= first[:, cols]) & (key_at <= query_at)
        bias[0:reach, :] = jnp.where(kept, 0.0, NEG)

        def one_head(h, unused):
            dims = pl.ds(pl.multiple_of(h * HEAD_DIM, HEAD_DIM), HEAD_DIM)
            tiles = [slice(t * KEY_TILE, (t + 1) * KEY_TILE) for t in range(reach // KEY_TILE)]

            def by_eight(tile):
                return tile.reshape(KEY_TILE // 8, 8, QUERY_BLOCK)

            query, out_grad = q_t[dims, cols], g_t[dims, cols]
            most = jnp.full((8, QUERY_BLOCK), NEG, F32)
            for keys in tiles:
                scores = dot_nn(k_n[h, keys, :], query) + bias[keys, :]
                expo[keys, :] = scores
                most = jnp.maximum(most, jnp.max(by_eight(scores), axis=0))
            most = jnp.max(most, axis=0, keepdims=True)
            total = jnp.zeros((8, QUERY_BLOCK), F32)
            centre = jnp.zeros((8, QUERY_BLOCK), F32)
            for keys in tiles:
                exponent = jnp.exp(expo[keys, :] - most)
                grads = dot_nn(v_n[h, keys, :], out_grad)
                expo[keys, :] = exponent
                prob_grad[keys, :] = grads
                total = total + jnp.sum(by_eight(exponent), axis=0)
                centre = centre + jnp.sum(by_eight(exponent * grads), axis=0)
            scale_by = 1.0 / jnp.sum(total, axis=0, keepdims=True)
            centre = jnp.sum(centre, axis=0, keepdims=True) * scale_by
            for keys in tiles:
                prob = expo[keys, :] * scale_by
                prob_low[keys, :] = prob.astype(BF16)
                score_low[keys, :] = (prob * (prob_grad[keys, :] - centre)).astype(BF16)
            o_t[dims, cols] = dot_nn(v_t[dims, 0:reach], prob_low[0:reach, :]).astype(BF16)
            dq_n[h, cols, :] = dot_nn(k_t[dims, 0:reach], score_low[0:reach, :]).T
            dk[h, 0:reach, :] += dot_nn(score_low[0:reach, :], q_n[h, cols, :])
            dv[h, 0:reach, :] += dot_nn(prob_low[0:reach, :], g_n[h, cols, :])
            return unused

        lax.fori_loop(0, heads, one_head, 0)

    blocks = length // ROWS_STEP

    def rows_at(b):
        return pl.ds(pl.multiple_of(b * ROWS_STEP, ROWS_STEP), ROWS_STEP)

    def back_copy(b):
        return remote(back.at[rows_at(b)], back_got.at[rows_at(b)], pass_sems, b, other_core)

    def branch_copy(b):
        there = branch_got.at[rows_at(b)]
        return remote(branch.at[rows_at(b)], there, pass_sems, blocks + b, other_core)

    def partials(b, unused):
        rows = rows_at(b)
        for target, source in ((dq_low, dq_n), (dk_low, dk), (dv_low, dv)):
            joined = jnp.concatenate([source[h, rows, :] for h in range(heads)], axis=1)
            target[rows, :] = joined.astype(BF16)
        total = dot_nt(dq_low[rows, :], wq[...]) + dot_nt(dk_low[rows, :], wk[...])
        back[rows, :] = (total + dot_nt(dv_low[rows, :], wv[...])).astype(BF16)
        back_copy(b).start()
        branch[rows, :] = dot_tn(o_t[:, rows], wm[...]).astype(BF16)
        branch_copy(b).start()
        return unused

    lax.fori_loop(0, blocks, partials, 0)
    cut = width // 2
    attn_rows = width + cut + head_cols
    pack[0:width, 0:head_cols] = dot_tn(normed[...], dq_low[...]).astype(BF16)
    pack[0:width, head_cols:] = dot_tn(normed[...], dk_low[...]).astype(BF16)
    value_grad = dot_tn(normed[...], dv_low[...]).astype(BF16)
    pack[width : width + cut, 0:head_cols] = value_grad[:cut]
    pack[width : width + cut, head_cols:] = value_grad[cut:]
    pack[width + cut : attn_rows, :] = dot_nn(o_t[...], grad[...]).astype(BF16)
    for load in loads[5:]:
        load.wait()
    gout[...] = jnp.zeros_like(gout)
    ggate[...] = jnp.zeros_like(ggate)
    gain_grad_o[...] = jnp.zeros_like(gain_grad_o)

    def stores(b):
        rows = rows_at(b)
        return [
            pltpu.make_async_copy(source.at[rows], target.at[rows], store_sems.at[i, b])
            for i, (source, target) in enumerate(
                ((base, base_o), (scan_grad, scan_grad_o), (gate_back, back_o))
            )
        ]

    def gating(b, unused):
        rows = rows_at(b)
        back_copy(b).wait()
        branch_copy(b).wait()
        middle = x[rows, :].astype(F32) + (part_a[rows, :].astype(F32) + part_b[rows, :].astype(F32))
        total = back[rows, :].astype(F32) + back_got[rows, :].astype(F32)
        factor = rms_scale(middle)
        middle_grad = grad[rows, :].astype(F32) + rms_back(middle, factor, gain[...], total)
        gain_grad_o[...] += jnp.sum(total * middle * factor, axis=0, keepdims=True)
        layer_out = middle + (branch[rows, :].astype(F32) + branch_got[rows, :].astype(F32))
        chosen = (1 - core).astype(F32)
        base[rows, :] = chosen * middle_grad + (1.0 - chosen) * layer_out
        low = middle_grad.astype(BF16)
        gout[...] += dot_tn(gated[rows, :], low)
        gated_grad = dot_nt(low, out_w[...])
        z = gate[rows, :]
        sigma = jax.nn.sigmoid(z)
        scan_grad[rows, :] = gated_grad * (z * sigma)
        slope = sigma * (1.0 + z * (1.0 - sigma))
        gate_low = (gated_grad * scan_out[rows, :] * slope).astype(BF16)
        ggate[...] += dot_tn(normed_a[rows, :], gate_low)
        gate_back[rows, :] = dot_nt(gate_low, w_gate[...])
        for store in stores(b):
            store.start()
        return unused

    lax.fori_loop(0, blocks, gating, 0)
    pack[attn_rows : attn_rows + channels, :] = gout[...].astype(BF16)
    pack[attn_rows + channels :, :] = ggate[...].astype(BF16)
    last = pltpu.make_async_copy(pack, pack_o, load_sems.at[0])
    last.start()
    for b in range(blocks):
        for store in stores(b):
            store.wait()
    last.wait()


def scan_back_block(
    coef, pre, step_in, scan_grad, flags, starts, step_w, decay_t, skip,
    act_grad, coef_grad, small, spare, between,
):
    (state, steps, stepd, drive, reads, blocked, d_drive, d_expo, in_own, read_own,
     decays, decayed, h_low, sum_low, expo_low) = spare
    block, width = pre.shape
    states = decay_t.shape[0]
    rank = step_w.shape[0]
    tiles = width // 128
    wide = CHUNK * states

    step_pre = step_in[...]
    step = softplus(step_pre)
    act = pre[...] * jax.nn.sigmoid(pre[...])
    spread(steps, step)
    spread(drive, step * act)
    spread(stepd, jnp.where(flags[:, 1:2] > 0.0, step, FAR))
    spread(reads, scan_grad[...])
    neg = -jnp.exp(decay_t[...])
    neg_of = [neg[:, c * 128 : (c + 1) * 128] for c in range(tiles)]
    picks = state_picks(CHUNK, states)
    own = own_token(CHUNK, states)
    own_low = own.astype(F32).astype(BF16)
    own_all = jnp.concatenate([own] * (block // CHUNK), axis=0)
    blocked[...] = jnp.where(
        own_all, dot_tn(coef[rank : rank + states, :].astype(BF16), picks), 0.0
    ).astype(BF16)

    def one_chunk(i, backward, spare):
        decay_s, decayed_s, h_s, sum_s, expo_s = spare
        rows16 = pl.ds(pl.multiple_of(i * CHUNK, CHUNK), CHUNK)
        tile = coef[rank:, pl.ds(pl.multiple_of((i // 8) * 128, 128), 128)]
        tile = pltpu.roll(tile, lax.rem(128 - lax.rem(i, 8) * CHUNK, 128), 1)
        h = [starts[rows16, c * 128 : (c + 1) * 128] for c in range(tiles)]
        for at in range(CHUNK):
            row = i * CHUNK + at
            here = slice(at * states, (at + 1) * states)
            write = column_of(tile[:states], at)
            for c in range(tiles):
                cols = slice(c * 128, (c + 1) * 128)
                decay = jnp.exp(neg_of[c] * row_of(stepd, c, row, states))
                kept = decay * h[c]
                h[c] = kept + row_of(drive, c, row, states) * write
                decay_s[c, here, :] = decay
                decayed_s[c, here, :] = kept
                h_s[here, cols] = h[c].astype(BF16)
        total = [jnp.zeros((states, 128), F32)] * tiles
        for at in reversed(range(CHUNK)):
            row = i * CHUNK + at
            here = slice(at * states, (at + 1) * states)
            read = column_of(tile[states:], at)
            for c in range(tiles):
                cols = slice(c * 128, (c + 1) * 128)
                summed = read * row_of(reads, c, row, states) + backward[c]
                sum_s[here, cols] = summed.astype(BF16)
                expo = summed * decayed_s[c, here, :]
                expo_s[here, cols] = (expo * neg_of[c]).astype(BF16)
                total[c] = total[c] + expo * row_of(steps, c, row, states)
                backward[c] = decay_s[c, here, :] * summed
        for c in range(tiles):
            small[rank : rank + states, c * 128 : (c + 1) * 128] += total[c]

        def flat(ref):
            return jnp.concatenate([ref[c, rows16, :] for c in range(tiles)], axis=1).astype(BF16)

        d_drive[rows16, :] = dot_nn(blocked[rows16, :], sum_s[...])
        d_expo[rows16, :] = dot_nn(own_low, expo_s[...])
        in_own[rows16, :] = jnp.where(own, dot_nt(flat(drive), sum_s[...]), 0.0)
        read_own[rows16, :] = jnp.where(own, dot_nt(flat(reads), h_s[...]), 0.0)
        return backward

    def pair(step_no, carried):
        between(step_no)
        backward = list(carried)
        last = block // CHUNK - 1 - 2 * step_no
        for sub in range(2):
            spare = (decays.at[sub], decayed.at[sub], h_low.at[sub], sum_low.at[sub], expo_low.at[sub])
            backward = one_chunk(last - sub, backward, spare)
        return tuple(backward)

    begin = tuple(state[:, c * 128 : (c + 1) * 128] for c in range(tiles))
    for c, last in enumerate(lax.fori_loop(0, block // (2 * CHUNK), pair, begin)):
        state[:, c * 128 : (c + 1) * 128] = last

    def by_state(ref):
        high = ref[...].astype(BF16)
        rest = (ref[...] - high.astype(F32)).astype(BF16)
        return dot_nt(picks, high) + dot_nt(picks, rest)

    coef_grad[rank : rank + states, :] = by_state(in_own)
    coef_grad[rank + states :, :] = by_state(read_own)

    drive_grad = d_drive[...]
    pre_grad = (d_expo[...] + drive_grad * act) * jax.nn.sigmoid(step_pre)
    tail = rank + states
    small[tail : tail + 1, :] += jnp.sum(pre_grad, axis=0, keepdims=True)
    pre_low = pre_grad.astype(BF16)
    small[:rank, :] += dot_nn(coef[:rank, :].astype(BF16), pre_low)
    coef_grad[:rank, :] = dot_nt(step_w[...], pre_low)
    act_grad[...] = drive_grad * step + scan_grad[...] * skip[...]
    small[tail + 1 : tail + 2, :] += jnp.sum(scan_grad[...] * act, axis=0, keepdims=True)


def conv_back_block(
    coef_grad, pre, act_grad, conv_in, normed, x, gate_back, flags, state_w, taps, w_conv,
    ext, gconv, gsmall, taps_at,
):
    block = pre.shape[0]
    coefs = coef_grad.shape[0]
    v = pre[...]
    sigma = jax.nn.sigmoid(v)
    gsmall[0:coefs, :] += dot_nn(coef_grad, (v * sigma).astype(BF16))
    act_all = act_grad[...] + dot_tn(coef_grad, state_w[...])
    conv_grad = act_all * (sigma * (1.0 + v * (1.0 - sigma)))
    ext[0:block, :] = conv_grad
    conv_in_grad = taps[3:4, :] * conv_grad
    sums = [None] * 4
    sums[3] = jnp.sum(conv_grad * conv_in[...], axis=0, keepdims=True)
    for j in range(1, 4):
        moved = jnp.where(flags[:, 4 + j : 5 + j] > 0.0, ext[j : j + block, :], 0.0)
        sums[3 - j] = jnp.sum(moved * conv_in[...], axis=0, keepdims=True)
        conv_in_grad = conv_in_grad + taps[3 - j : 4 - j, :] * moved
    for j in range(4):
        gsmall[taps_at + j : taps_at + j + 1, :] += sums[j]
    gsmall[taps_at + 4 : taps_at + 5, :] += jnp.sum(conv_grad, axis=0, keepdims=True)
    low = conv_in_grad.astype(BF16)
    gconv[...] += dot_tn(normed[...], low)
    back = gate_back[...] + dot_nt(low, w_conv[...])
    u = x[...].astype(F32)
    gsmall[taps_at + 5 : taps_at + 6, :] += jnp.sum(back * u * rms_scale(u), axis=0, keepdims=True)
    ext[block:, :] = ext[0:8, :]
    return back


def sum_plan(rows, counts):
    bits = [(axis, 1 << i) for axis, size in counts for i in range(size.bit_length() - 1)]
    digits = [bits[i : i + 2] for i in range(0, len(bits), 2)]
    most = (rows * 13 // 20 + 128) // 256 * 256
    sizes = [(0, most), (1, rows - most)] if rows > 1024 else [(0, most // 2), (0, most // 2), (1, rows - most)]
    streams, at, land = [], 0, 0
    for number, size in sizes:
        turn = number % len(digits)
        steps, held = [], size
        for digit in digits[turn:] + digits[:turn]:
            radix = 1 << len(digit)
            split = held % (16 * radix) == 0
            held = held // radix if split else held
            steps.append((digit, split, held, land))
            land += held * (radix - 1)
        streams.append((at, size, steps))
        at += size
    return streams, land


class Summing:
    def __init__(self, plan, src, work, land, full, peer, send, recv):
        self.streams, self.src, self.work, self.land = plan, src, work, land
        self.full, self.peer = full, peer
        self.sems = (send, recv)
        self.turns = len(plan[0][2])
        self.phases = 2 * self.turns + 2
        self.start = []
        for first, _, steps in plan:
            at, spots = first, [first]
            for turn, (digit, split, kept, _) in enumerate(steps):
                at = at + self.index(digit, 0) * kept if split else at
                spots.append(at)
            self.start.append(spots)

    def index(self, digit, flipped):
        total = 0
        for i, (axis, weight) in enumerate(digit):
            place = lax.rem(lax.axis_index(axis) // weight, 2)
            total = total + (1 - place if flipped >> i & 1 else place) * (1 << i)
        return total

    def partner(self, digit, flipped):
        device = {}
        for i, (axis, weight) in enumerate(digit):
            if flipped >> i & 1:
                me = lax.axis_index(axis)
                device[axis] = device.get(axis, me) + weight * (1 - 2 * lax.rem(me // weight, 2))
        return device

    def other_core(self):
        return {"kind": 1 - lax.axis_index("kind")}

    def others(self, s, turn):
        return range(1, 1 << len(self.streams[s][2][turn][0]))

    def rows(self, ref, at, size):
        return ref.at[pl.ds(pl.multiple_of(at, 16), size)]

    def number(self, s, kind, turn, flipped):
        return ((s * 3 + kind) * (self.turns + 1) + turn) * 4 + flipped

    def piece(self, s, turn, flipped):
        digit, split, kept, _ = self.streams[s][2][turn]
        at = self.start[s][turn]
        return at + self.index(digit, flipped) * kept if split else at

    def halves(self, s, turn):
        digit, _, kept, land = self.streams[s][2][turn]
        source = self.src if turn == 0 else self.work
        return [
            remote(
                self.rows(source, self.piece(s, turn, q), kept),
                self.land.at[pl.ds(land + (q - 1) * kept, kept)],
                self.sems, self.number(s, 0, turn, q), self.partner(digit, q),
            )
            for q in self.others(s, turn)
        ]

    def add(self, s, turn):
        _, _, kept, land = self.streams[s][2][turn]
        at = self.start[s][turn + 1]
        source = self.src if turn == 0 else self.work
        target = self.full if turn == self.turns - 1 else self.work

        def step(i, unused):
            here = pl.ds(pl.multiple_of(at + i * 16, 16), 16)
            parts = [source[here, :].astype(F32)]
            for q in self.others(s, turn):
                there = pl.ds(pl.multiple_of(land + (q - 1) * kept + i * 16, 16), 16)
                parts.append(self.land[there, :].astype(F32))
            while len(parts) > 1:
                parts = [parts[i] + parts[i + 1] for i in range(0, len(parts), 2)]
            target[here, :] = parts[0].astype(BF16)
            return unused

        lax.fori_loop(0, kept // 16, step, 0)

    def spreads(self, s, turn):
        digit, split, kept, _ = self.streams[s][2][turn]
        if not split:
            return []
        here = self.rows(self.full, self.start[s][turn + 1], kept)
        return [
            remote(here, here, self.sems, self.number(s, 1, turn, q), self.partner(digit, q))
            for q in self.others(s, turn)
        ]

    def shares(self, s, turn):
        if turn == self.turns:
            found = [(0, self.start[s][turn], self.streams[s][2][-1][2])]
        else:
            _, split, kept, _ = self.streams[s][2][turn]
            found = [(q, self.piece(s, turn, q), kept) for q in self.others(s, turn)] if split else []
        return [
            remote(
                self.rows(self.full, at, size), self.rows(self.peer, at, size), self.sems,
                self.number(s, 2, turn, q), self.other_core(),
            )
            for q, at, size in found
        ]

    def slots(self, count):
        lengths = [2.5 + 14.0 * 0.5**turn for turn in range(self.turns)]
        found, at = [0], 0.0
        for length in lengths + lengths[::-1]:
            at += length * count / 42.0
            if at < count - 1:
                found.append(int(at))
        return found

    def greet(self):
        barrier = pltpu.get_barrier_semaphore()
        partners = [self.other_core()]
        for digit, _, _, _ in self.streams[0][2]:
            partners += [self.partner(digit, q) for q in range(1, 1 << len(digit))]
        for device in partners:
            pl.semaphore_signal(
                barrier, inc=1, device_id=device, device_id_type=pl.DeviceIdType.MESH
            )
        pl.semaphore_wait(barrier, len(partners))

    def begin(self, copies):
        for copy in copies:
            copy.start()

    def finish(self, copies):
        for copy in copies:
            copy.wait()

    def phase(self, number):
        for s in range(len(self.streams)):
            if number == 0:
                self.begin(self.halves(s, 0))
            elif number <= self.turns:
                self.finish(self.halves(s, number - 1))
                self.add(s, number - 1)
                if number < self.turns:
                    self.begin(self.halves(s, number))
                else:
                    self.begin(self.spreads(s, self.turns - 1))
                    self.begin(self.shares(s, self.turns))
            elif number <= 2 * self.turns:
                turn = 2 * self.turns - number
                self.finish(self.spreads(s, turn))
                if turn > 0:
                    self.begin(self.spreads(s, turn - 1))
                self.begin(self.shares(s, turn))
            else:
                for turn in range(self.turns + 1):
                    self.finish(self.shares(s, turn))


def sum_scratch(plan, rows, land, width):
    numbers = len(plan) * 3 * (len(plan[0][2]) + 1) * 4
    return [
        pltpu.VMEM((rows, width), BF16),
        pltpu.VMEM((land, width), BF16),
        pltpu.VMEM((rows, width), BF16),
        pltpu.VMEM((rows, width), BF16),
        pltpu.SemaphoreType.DMA((numbers,)),
        pltpu.SemaphoreType.DMA((numbers,)),
    ]


def both_copies(summing, out, sems, number):
    core = lax.axis_index("kind")
    return [
        pltpu.make_async_copy(summing.full, out.at[core], sems.at[number]),
        pltpu.make_async_copy(summing.peer, out.at[1 - core], sems.at[number + 1]),
    ]


def back_kernel(
    plan, plan_last, steps,
    coef, pre, step_in, scan_grad, flags, starts,
    pre_late, conv_in, normed, x, gate_back, flags_late,
    gain, gain_grad, pack, x_all, base_all, weights_all,
    early_o, late_o, kept_o, got_o,
    step_w, decay_t, skip, state_w, taps, w_conv, weight_sems,
    scan_spare, small, act_grads, coef_grads, coef_got, ext, gconv, gsmall, back, low, low_got,
    x_s, base_s, kept, sent, got, pack_last, sum_spare, sum_spare_last,
    coef_sems, low_sems, pass_sems, local_sems,
):
    pid = pl.program_id(0)
    states, rank, coefs = decay_t.shape[0], step_w.shape[0], state_w.shape[0]
    block = pre.shape[0]
    pairs = block // (2 * CHUNK)
    taps_at = coefs + small.shape[0]
    core, row = lax.axis_index("kind"), lax.axis_index("inner")
    other_core = {"kind": 1 - core}
    first_sum = Summing(plan, pack, *sum_spare)
    last_sum = Summing(plan_last, pack_last, *sum_spare_last)
    slots = first_sum.slots(pairs * steps)
    load_x = pltpu.make_async_copy(x_all, x_s, local_sems.at[0])
    load_base = pltpu.make_async_copy(base_all, base_s, local_sems.at[1])
    mine = pl.ds(pl.multiple_of(core * w_conv.shape[1], 128), w_conv.shape[1])
    load_weights = [
        pltpu.make_async_copy(source.at[:, mine], target, weight_sems.at[i])
        for i, (source, target) in enumerate(
            zip(weights_all, (step_w, decay_t, skip, state_w, taps, w_conv), strict=True)
        )
    ]

    def coef_copy(i):
        return remote(coef_grads.at[i], coef_got.at[i], coef_sems, i, other_core)

    def low_copy(i):
        here = pl.ds(pl.multiple_of((steps - 1 - i) * block, block), block)
        return remote(low.at[here], low_got.at[here], low_sems, i, other_core)

    def first_phase(number):
        first_sum.phase(number)

    @pl.when(pid == 0)
    def _():
        scan_spare[0][...] = jnp.zeros_like(scan_spare[0])
        small[...] = jnp.zeros_like(small)
        ext[block:, :] = jnp.zeros((8, ext.shape[1]), F32)
        gconv[...] = jnp.zeros_like(gconv)
        gsmall[...] = jnp.zeros_like(gsmall)
        for copy in load_weights:
            copy.start()
        first_sum.greet()
        load_x.start()
        load_base.start()
        for copy in load_weights:
            copy.wait()

    @pl.when(pid < steps)
    def _():
        def between(step_no):
            slot = pid * pairs + step_no
            for number, at in enumerate(slots):
                pl.when(slot == at)(functools.partial(first_phase, number))

        scan_back_block(
            coef, pre, step_in, scan_grad, flags, starts, step_w, decay_t, skip,
            act_grads.at[lax.rem(pid, 2)], coef_grads.at[pid], small, scan_spare, between,
        )
        coef_copy(pid).start()

    @pl.when(pid > 0)
    def _():
        late = pid - 1
        coef_copy(late).wait()
        coef_low = (coef_grads[late] + coef_got[late]).astype(BF16)
        here = pl.ds(pl.multiple_of((steps - 1 - late) * block, block), block)
        part = conv_back_block(
            coef_low, pre_late, act_grads.at[lax.rem(late, 2)], conv_in, normed, x, gate_back,
            flags_late, state_w, taps, w_conv, ext, gconv, gsmall, taps_at,
        )
        back[here, :] = part
        low[here, :] = part.astype(BF16)
        low_copy(late).start()

    @pl.when(pid == steps)
    def _():
        width = gconv.shape[0]
        small[rank : rank + states, :] = small[rank : rank + states, :] * -jnp.exp(decay_t[...])
        gsmall[coefs:taps_at, :] = small[...]
        gsmall[taps_at + 6 : taps_at + 7, :] = gain_grad[...]
        pack_last[0:width, :] = gconv[...].astype(BF16)
        pack_last[width:, :] = gsmall[...].astype(BF16)
        last_sum.phase(0)
        for i in range(steps):
            low_copy(i).wait()
        load_x.wait()
        load_base.wait()
        chosen = (1 - core).astype(F32)
        half = kept.shape[0]

        def finish(at, target):
            def part(i, unused):
                here = pl.ds(pl.multiple_of(at + i * 64, 64), 64)
                there = pl.ds(pl.multiple_of(i * 64, 64), 64)
                u = x_s[here, :].astype(F32)
                total = back[here, :] + low_got[here, :].astype(F32)
                backward = rms_back(u, rms_scale(u), gain[...], total)
                target[there, :] = (base_s[here, :] + chosen * backward).astype(target.dtype)
                return unused

            lax.fori_loop(0, half // 64, part, 0)

        finish((1 - row) * half, sent)
        pieces = last_sum.phases - 2
        passing = [
            remote(
                sent.at[pl.ds(i * (half // pieces), half // pieces)],
                got.at[pl.ds(i * (half // pieces), half // pieces)], pass_sems, i, {"inner": 1 - row},
            )
            for i in range(pieces)
        ]
        finish(row * half, kept)
        keep = pltpu.make_async_copy(kept, kept_o, local_sems.at[2])
        keep.start()
        for number in range(len(slots), first_sum.phases):
            first_sum.phase(number)
        store_first = both_copies(first_sum, early_o, local_sems, 3)
        for copy in store_first:
            copy.start()
        for number in range(1, last_sum.phases):
            last_sum.phase(number)
            if number <= pieces:
                passing[number - 1].start()
        store_last = both_copies(last_sum, late_o, local_sems, 5)
        for copy in passing:
            copy.wait()
        store_got = pltpu.make_async_copy(got, got_o, local_sems.at[7])
        store_got.start()
        for copy in store_last:
            copy.start()
        for copy in store_first + store_last + [keep, store_got]:
            copy.wait()


def assemble_kernel(
    sizes, sel, kept, got, query_key, value, mixed, out, gate, conv, small,
    results_o, in_o, out_o, query_o, key_o, value_o, mixed_o,
    state_o, step_o, decay_o, step_bias_o, skip_o, taps_o, conv_bias_o, gain_o, attn_gain_o,
):
    first = sel[1] == 0
    mine, other = kept[...], got[...].astype(F32)
    results_o[0, 0] = jnp.where(first, mine, other)
    results_o[0, 1] = jnp.where(first, other, mine)
    half = conv.shape[2]
    cut = query_key.shape[2] // 2
    for part in range(2):
        here = slice(part * cut, (part + 1) * cut)
        in_o[:, part * half : (part + 1) * half] = conv[part].astype(F32)
        in_o[:, (2 + part) * half : (3 + part) * half] = gate[part].astype(F32)
        query_o[:, here] = query_key[part, :, :cut].astype(F32)
        key_o[:, here] = query_key[part, :, cut:].astype(F32)
        value_o[0, :, here] = value[part, :, :cut].astype(F32)
        value_o[1, :, here] = value[part, :, cut:].astype(F32)
    out_o[...] = out[...].astype(F32)
    mixed_o[...] = mixed[...].astype(F32)
    both = jnp.concatenate([small[0].astype(F32), small[1].astype(F32)], axis=1)
    coefs, rank, states = sizes
    at = 0
    for target, size in (
        (state_o, coefs), (step_o, rank), (decay_o, states), (step_bias_o, 1), (skip_o, 1),
        (None, 6), (taps_o, 4), (conv_bias_o, 1),
    ):
        if target is not None:
            target[...] = both[at : at + size]
        at += size
    gain_o[...] = both[at : at + 1, :half] + both[at : at + 1, half:]
    attn_gain_o[...] = both[at + 1 : at + 2, :half]


def local(
    layer_input, output_grad, document_ids, mamba_gain, in_proj, conv_weight, conv_bias, state_proj,
    step_proj, step_bias, decay_log, skip_gain, out_proj, attn_gain, query_proj, key_proj, value_proj,
    mixed_proj,
):
    _, piece_len, width = layer_input.shape
    length = output_grad.shape[1]
    parts = lax.axis_size("kind")
    half = in_proj.shape[1] // (2 * parts)
    states = decay_log.shape[1]
    rank = step_proj.shape[0]
    coefs = state_proj.shape[1]
    head_cols = width // parts
    heads = head_cols // HEAD_DIM
    core = lax.axis_index("kind")
    row = lax.axis_index("inner")
    sel = jnp.stack([core, row]).astype(jnp.int32)
    steps = length // ROWS_STEP

    def swap(value, axis):
        return jax.tree.map(lambda v: lax.ppermute(v, axis, [(0, 1), (1, 0)]), value)

    ids = lax.dynamic_index_in_dim(document_ids, row, 0, keepdims=False)
    first = jnp.sum((ids[None, :] < ids[:, None]).astype(jnp.int32), axis=1)
    since = jnp.arange(length, dtype=jnp.int32) - first
    after = jnp.concatenate([since, jnp.zeros((4,), jnp.int32)])
    flags = jnp.stack(
        [since >= j for j in range(4)] + [after[j : j + length] >= max(j, 1) for j in range(4)],
        axis=1,
    ).astype(F32)
    first = first[None, :]
    taps = conv_weight.T
    state_t = state_proj.T
    decay_t = decay_log.T
    conv_b, step_b, skip = conv_bias[None, :], step_bias[None, :], skip_gain[None, :]
    gain_a, gain_b = mamba_gain[None, :], attn_gain[None, :]

    def rows(array):
        return (array, (ROWS_STEP, array.shape[1]), lambda i, sel: (i, 0))

    def rows_rev(array):
        return (array, (ROWS_STEP, array.shape[1]), lambda i, sel: (steps - 1 - i, 0))

    def cols(array):
        return (array, (array.shape[0], ROWS_STEP), lambda i, sel: (0, i))

    def cols_rev(array):
        return (array, (array.shape[0], ROWS_STEP), lambda i, sel: (0, steps - 1 - i))

    def full(array):
        return (array,) + whole(array.shape)

    def half_cols(array, size, shift=0):
        return (array, (array.shape[0], size), lambda i, sel: (0, sel[0] + shift))

    def half_rows(array, size):
        return (array, (size, array.shape[1]), lambda i, sel: (sel[0], 0))

    def out_rows(size, dtype):
        return ((length, size), dtype, (ROWS_STEP, size), lambda i, sel: (i, 0))

    def out_rows_rev(size, dtype):
        return ((length, size), dtype, (ROWS_STEP, size), lambda i, sel: (steps - 1 - i, 0))

    def out_whole(shape, dtype=F32):
        return (shape, dtype) + whole(shape)

    w_conv = half_cols(in_proj, half)
    w_gate = half_cols(in_proj, half, parts)
    taps_half = half_cols(taps, half)
    state_half = half_cols(state_t, half)
    step_half = half_cols(step_proj, half)
    decay_half = half_cols(decay_t, half)
    skip_half = half_cols(skip, half)
    out_half = half_rows(out_proj, half)

    small_rows = rank + states + 8
    block_f32 = pltpu.VMEM((half // 128, ROWS_STEP, 128), F32)
    plain_f32 = pltpu.VMEM((ROWS_STEP, half), F32)
    wide = CHUNK * states
    blocks = length // ROWS_STEP
    assert length // CHUNK * states == length
    row_outs = [
        (width, BF16), (width, BF16), (half, F32), (half, F32), (half, F32), None, (half, F32), (half, F32),
        (half, BF16), (half, F32), (width, BF16), (width, BF16),
    ]
    row_f32, row_low = pltpu.VMEM((length, half), F32), pltpu.VMEM((length, half), BF16)
    x_low = pltpu.VMEM((length, width), BF16)
    block_coef = (blocks, coefs, ROWS_STEP)
    front_weights = (in_proj, state_t, step_proj, decay_t, skip, taps, conv_b, step_b, out_proj)

    def pair_of_sems(count):
        return [pltpu.SemaphoreType.DMA((count,)), pltpu.SemaphoreType.DMA((count,))]

    (x, normed_a, conv_in, conv_pre, gate_z, coef, step_pre, scan_out, gated, starts, branch,
     branch_other) = pl.pallas_call(
        front_kernel,
        in_specs=[pl.BlockSpec(memory_space=pltpu.VMEM)] * 2 + [pl.BlockSpec(memory_space=pl.ANY)]
        + [(pl.BlockSpec(memory_space=pl.ANY),) * len(front_weights)],
        out_specs=[pl.BlockSpec(memory_space=pl.ANY)] * len(row_outs),
        out_shape=[
            jax.ShapeDtypeStruct(block_coef, F32) if out is None
            else jax.ShapeDtypeStruct((length, out[0]), out[1])
            for out in row_outs
        ],
        scratch_shapes=[
            x_low, x_low, pltpu.VMEM((length + 8, half), F32), row_f32, row_f32,
            pltpu.VMEM(block_coef, F32), pltpu.VMEM(block_coef, F32), pltpu.VMEM(block_coef, F32),
            row_f32, row_f32, row_low, row_f32, x_low, x_low,
            [pltpu.VMEM((width, half), BF16), pltpu.VMEM((width, half), BF16)]
            + [pltpu.VMEM((array.shape[0], half), array.dtype)
               for array in (state_t, step_proj, decay_t, skip, taps, conv_b, step_b)]
            + [pltpu.VMEM((half, width), BF16)],
            [pltpu.VMEM((states, half), F32), block_f32, block_f32, plain_f32,
             pltpu.VMEM((ROWS_STEP, wide), BF16), pltpu.VMEM((STRETCH * wide, half), BF16)],
            pltpu.SemaphoreType.DMA((11,)), pair_of_sems(2), pair_of_sems(blocks), pair_of_sems(blocks),
            pltpu.SemaphoreType.DMA((9, blocks)), pltpu.SemaphoreType.DMA((3,)),
        ],
        compiler_params=pltpu.CompilerParams(
            vmem_limit_bytes=VMEM_BYTES, collective_id=2, has_side_effects=True
        ),
        cost_estimate=pl.CostEstimate(
            flops=2 * length * states * half * 1000, bytes_accessed=1 << 24, transcendentals=0
        ),
        name="front",
    )(flags, gain_a, layer_input, front_weights)

    vmem_spec = pl.BlockSpec(memory_space=pltpu.VMEM)
    any_spec = pl.BlockSpec(memory_space=pl.ANY)
    token_head = pltpu.VMEM((heads, length, HEAD_DIM), BF16)
    token_head_f32 = pltpu.VMEM((heads, length, HEAD_DIM), F32)
    head_token = pltpu.VMEM((head_cols, length), BF16)
    scores_f32 = pltpu.VMEM((length, QUERY_BLOCK), F32)
    scores_low = pltpu.VMEM((length, QUERY_BLOCK), BF16)
    tokens_low = pltpu.VMEM((length, width), BF16)
    tokens_f32 = pltpu.VMEM((length, width), F32)
    head_low = pltpu.VMEM((length, head_cols), BF16)
    square = pltpu.VMEM((width, head_cols), BF16)
    pack_rows = width + width // 2 + head_cols + half + width
    base, scan_grad, gate_back, pack_early, g_attn_gain = pl.pallas_call(
        middle_kernel,
        in_specs=[vmem_spec] * 5 + [any_spec] * 5 + [(any_spec,) * 6],
        out_specs=[any_spec] * 4 + [vmem_spec],
        out_shape=[
            jax.ShapeDtypeStruct((length, width), F32),
            jax.ShapeDtypeStruct((length, half), F32),
            jax.ShapeDtypeStruct((length, width), F32),
            jax.ShapeDtypeStruct((pack_rows, width), BF16),
            jax.ShapeDtypeStruct((1, width), F32),
        ],
        scratch_shapes=[
            tokens_low, pltpu.VMEM((length, half), BF16), pltpu.VMEM((length, half), F32),
            pltpu.VMEM((length, half), F32), tokens_low, square, square, square,
            pltpu.VMEM((head_cols, width), BF16), pltpu.VMEM((half, width), BF16),
            pltpu.VMEM((width, half), BF16),
            tokens_low, head_token, token_head, token_head, token_head, head_token, head_token,
            token_head, head_token, head_token, token_head_f32, token_head_f32, token_head_f32,
            scores_f32, scores_f32, scores_f32, scores_low, scores_low,
            head_low, head_low, head_low, tokens_low, tokens_low, tokens_low, tokens_low, tokens_f32,
            pltpu.VMEM((length, half), F32), tokens_f32, pltpu.VMEM((half, width), F32),
            pltpu.VMEM((width, half), F32), pltpu.VMEM((pack_rows, width), BF16),
            pltpu.SemaphoreType.DMA((11,)),
            [pltpu.SemaphoreType.DMA((2 * blocks,)), pltpu.SemaphoreType.DMA((2 * blocks,))],
            pltpu.SemaphoreType.DMA((3, blocks)),
        ],
        compiler_params=pltpu.CompilerParams(
            vmem_limit_bytes=VMEM_BYTES, collective_id=3, has_side_effects=True
        ),
        cost_estimate=pl.CostEstimate(
            flops=2 * length * length * width * 10, bytes_accessed=1 << 24, transcendentals=0
        ),
        name="middle",
    )(x, branch, branch_other, first, gain_b, output_grad, gated, gate_z, scan_out, normed_a,
      (query_proj, key_proj, value_proj, mixed_proj, out_proj, in_proj))

    counts = [("inner", lax.axis_size("inner")), ("dp", lax.axis_size("dp"))]
    plan, land = sum_plan(pack_early.shape[0], counts)
    last_rows = width + 128
    plan_last, land_last = sum_plan(last_rows, counts)
    tile_f32 = pltpu.VMEM((2, half // 128, wide, 128), F32)
    tile_low = pltpu.VMEM((2, wide, half), BF16)
    own_f32 = pltpu.VMEM((ROWS_STEP, wide), F32)

    def now(i):
        return jnp.maximum(steps - 1 - i, 0)

    def late_at(i):
        return jnp.minimum(steps - i, steps - 1)

    def back_rows(array, at):
        return (array, (ROWS_STEP, array.shape[1]), lambda i: (at(i), 0))

    def fixed(array):
        return (array, array.shape, None)

    ins = [
        (coef, (None, coefs, ROWS_STEP), lambda i: (now(i), 0, 0)), back_rows(conv_pre, now), back_rows(step_pre, now),
        back_rows(scan_grad, now), back_rows(flags, now),
        (starts, (ROWS_STEP // CHUNK * states, half), lambda i: (now(i), 0)),
        back_rows(conv_pre, late_at), back_rows(conv_in, late_at), back_rows(normed_a, late_at),
        back_rows(x, late_at), back_rows(gate_back, late_at), back_rows(flags, late_at),
        fixed(gain_a), fixed(g_attn_gain), fixed(pack_early),
    ]
    weights_all = (step_proj, decay_t, skip, state_t, taps, in_proj)
    specs = [
        pl.BlockSpec(block, lambda i: (0, 0), pipeline_mode=pl.Buffered(1)) if at is None
        else pl.BlockSpec(block, at)
        for _, block, at in ins
    ]
    early, late, kept, got = pl.pallas_call(
        functools.partial(back_kernel, plan, plan_last, steps),
        grid=(steps + 1,),
        in_specs=specs + [any_spec] * 2 + [(any_spec,) * len(weights_all)],
        out_specs=[any_spec] * 4,
        out_shape=[
            jax.ShapeDtypeStruct((parts,) + pack_early.shape, BF16),
            jax.ShapeDtypeStruct((parts, last_rows, width), BF16),
            jax.ShapeDtypeStruct((piece_len, width), F32),
            jax.ShapeDtypeStruct((piece_len, width), BF16),
        ],
        scratch_shapes=[pltpu.VMEM((array.shape[0], half), array.dtype) for array in weights_all] + [
            pltpu.SemaphoreType.DMA((len(weights_all),)),
            [pltpu.VMEM((states, half), F32), block_f32,
             block_f32, block_f32, block_f32, pltpu.VMEM((ROWS_STEP, wide), BF16), plain_f32,
             plain_f32, own_f32, own_f32, tile_f32, tile_f32, tile_low, tile_low, tile_low],
            pltpu.VMEM((small_rows, half), F32),
            pltpu.VMEM((2, ROWS_STEP, half), F32),
            pltpu.VMEM((steps, coefs, ROWS_STEP), F32),
            pltpu.VMEM((steps, coefs, ROWS_STEP), F32),
            pltpu.VMEM((ROWS_STEP + 8, half), F32),
            pltpu.VMEM((width, half), F32),
            pltpu.VMEM((128, half), F32),
            pltpu.VMEM((length, width), F32),
            pltpu.VMEM((length, width), BF16),
            pltpu.VMEM((length, width), BF16),
            pltpu.VMEM((length, width), BF16),
            pltpu.VMEM((length, width), F32),
            pltpu.VMEM((piece_len, width), F32),
            pltpu.VMEM((piece_len, width), BF16),
            pltpu.VMEM((piece_len, width), BF16),
            pltpu.VMEM((last_rows, width), BF16),
            sum_scratch(plan, pack_early.shape[0], land, width),
            sum_scratch(plan_last, last_rows, land_last, width),
            [pltpu.SemaphoreType.DMA((steps,)), pltpu.SemaphoreType.DMA((steps,))],
            [pltpu.SemaphoreType.DMA((steps,)), pltpu.SemaphoreType.DMA((steps,))],
            [pltpu.SemaphoreType.DMA((16,)), pltpu.SemaphoreType.DMA((16,))],
            pltpu.SemaphoreType.DMA((8,)),
        ],
        compiler_params=pltpu.CompilerParams(
            dimension_semantics=("arbitrary",), vmem_limit_bytes=VMEM_BYTES, collective_id=1,
            has_side_effects=True,
        ),
        cost_estimate=pl.CostEstimate(
            flops=2 * length * states * half * 3000, bytes_accessed=1 << 25, transcendentals=0
        ),
        name="back",
    )(*[a for a, _, _ in ins], x, base, weights_all)
    quarter = width // 4
    eighth = width // 8

    def from_sum(total, size, first_row):
        return (total, (parts, size, width), lambda i, sel: (0, first_row // size + i, 0))

    def out_parts(size):
        return ((parts, 4 * size, width), F32, (parts, size, width), lambda i, sel: (0, i, 0))

    attn_rows = width + width // 2 + head_cols
    results, t_in, t_out, t_query, t_key, t_value, t_mixed, *smalls = call(
        functools.partial(assemble_kernel, (coefs, rank, states)), sel, 4,
        [(kept, (piece_len // 4, width), lambda i, sel: (i, 0)),
         (got, (piece_len // 4, width), lambda i, sel: (i, 0)),
         from_sum(early, quarter, 0), from_sum(early, eighth, width),
         from_sum(early, eighth, width + width // 2), from_sum(early, quarter, attn_rows),
         from_sum(early, quarter, attn_rows + half), from_sum(late, quarter, 0),
         (late, (parts, 128, width), lambda i, sel: (0, width // 128, 0))],
        [((1, 2, piece_len, width), F32, (1, 2, piece_len // 4, width), lambda i, sel: (0, 0, i, 0)),
         ((width, 4 * half), F32, (quarter, 4 * half), lambda i, sel: (i, 0)),
         out_parts(quarter), ((width, width), F32, (quarter, width), lambda i, sel: (i, 0)),
         ((width, width), F32, (quarter, width), lambda i, sel: (i, 0)), out_parts(eighth),
         out_parts(eighth)]
        + [out_whole((size, parts * half)) for size in (coefs, rank, states, 1, 1, 4, 1)]
        + [out_whole((1, width))] * 2,
        [], 0, "assemble",
    )
    t_state, t_step, t_decay, t_step_bias, t_skip, t_taps, t_conv_bias, t_gain, t_attn_gain = smalls
    return (
        results, t_gain[0], t_in, t_taps.T, t_conv_bias[0], t_state.T, t_step, t_step_bias[0],
        t_decay.T, t_skip[0], t_out.reshape(out_proj.shape), t_attn_gain[0], t_query, t_key,
        t_value.reshape(width, width), t_mixed.reshape(width, width),
    )


def solution(mesh):
    in_specs = (P("dp", "inner", None), P("dp", None, None), P("dp", None)) + (P(),) * 15
    out_specs = (P("kind", "dp", "inner", None),) + (P(),) * 15
    return jax.shard_map(local, mesh=mesh, in_specs=in_specs, out_specs=out_specs, check_vma=False)
```

profile of v0, /device:TPU:0, one launch (start us, length us, event | category | flops | bytes accessed | tf_op | source)
XLA Modules:
  0.0 177.4 jit_solution(3106415398975017694)
XLA Ops:
  0.6 0.0 copy-start
  0.7 0.6 pad_add_fusion.sel
  1.2 0.1 copy-done
  1.4 0.6 convert_reduce_fusion
  1.9 0.0 copy-start.1
  1.9 0.1 fusion.2
  2.1 0.1 stack.32
  2.2 0.3 copy.39
  2.4 0.8 convert_element_type.7.flags.flags_late
  3.3 36.2 %front.1 = (bf16[1024,512]{1,0:T(8,128)(2,1)}, bf16[1024,512]{1,0:T(8,128)(2,1)}, f32[1024,512]{1,0:T(8,128)}, f32[1024,512]{1,0:T(8,128)}, f32[1024,512]{1,0:T(...) custom-call(f32[1024,8]{1,0:T(8,128)} %convert_element_type.7.flags., ...), custom_call_target="tpu_custom_call" | custom-call | flops 16777216000 | bytes 16777216 | tf_op jit(solution)/shard_map/front/pallas_call | solution.py:1097
  39.4 0.0 copy-done.1
  39.5 34.0 %middle.1 = (f32[1024,512]{1,0:T(8,128)}, f32[1024,512]{1,0:T(8,128)}, f32[1024,512]{1,0:T(8,128)}, bf16[2048,512]{1,0:T(8,128)(2,1)}, f32[1,512]{1,0:T(1,128)}) custom-call(bf16[1024,512]{1,0:T(8,128)(2,1)} %get-tuple-element.56.x.x_all, bf16[1024,512]{1,0:T(8,128)(2,1)} %get-tuple-element.57.part_a, bf16[1024,512]{1,0:T(8,128)(2,1)} %get-tuple-element.58.part_b, ...), custom_call_target="tpu_custom_call" | custom-call | flops 10737418240 | bytes 16777216 | tf_op jit(solution)/shard_map/middle/pallas_call | solution.py:1141
  73.4 94.6 %back.1 = (bf16[2,2048,512]{2,1,0:T(8,128)(2,1)}, bf16[2,640,512]{2,1,0:T(8,128)(2,1)}, f32[512,512]{1,0:T(8,128)}, bf16[512,512]{1,0:T(8,128)(2,1)}) custom-call(f32[4,64,256]{2,1,0:T(8,128)} %get-tuple-element.53.coef, f32[1024,512]{1,0:T(8,128)} %get-tuple-element.54.pre.pre_late, f32[1024,512]{1,0:T(8,128)} %get-tuple-element.55.step_in, ...), custom_call_target="tpu_custom_call" | custom-call | flops 50331648000 | bytes 33554432 | tf_op jit(solution)/shard_map/back/pallas_call | solution.py:1211
  168.0 9.2 %assemble.1 = (f32[1,2,512,512]{3,2,1,0:T(8,128)}, f32[512,2048]{1,0:T(8,128)}, f32[2,512,512]{2,1,0:T(8,128)}, f32[512,512]{1,0:T(8,128)}, f32[512,512]{1,0:T(8...) custom-call(s32[2]{0:T(128)} %pad_add_fusion.sel, ...), custom_call_target="tpu_custom_call" | custom-call | bytes 25165824 | tf_op jit(solution)/shard_map/assemble/pallas_call | solution.py:90
  (6 shorter events, 0.1 us)
Async XLA Ops:
  0.6 0.7 copy-start
  1.9 37.5 %copy-start.1 = (s32[1024]{0:T(1024)}, s32[1024]{0:T(1024)S(1)}, u32[]{:S(2)}) copy-start(s32[1024]{0:T(1024)S(1)} %convert_reduce_fusion) | copy-start | bytes 12292
where the time goes:
time: 178 us; the launch traced here: 177 us
  Pallas kernels  174 us (98%)
  other arithmetic  2.07 us (1%)
    pallas_call x1, Pallas kernels, local(): pl.pallas_call(functools.partial(back_kernel, plan, plan_last, steps), gr...  94.6 us
    pallas_call x1, Pallas kernels, local(): pl.pallas_call(front_kernel, in_specs=[pl.BlockSpec(memory_space=pltpu.VM...  36.2 us
    pallas_call x1, Pallas kernels, local(): pl.pallas_call(middle_kernel, in_specs=[vmem_spec] * 5 + [any_spec] * 5 +...  34 us
    pallas_call x1, Pallas kernels, call(): pl.pallas_call(body, grid_spec=pltpu.PrefetchScalarGridSpec(num_scalar_pr...  9.22 us

commit v1 on v0

--- a/solution.py
+++ b/solution.py
@@ -303,13 +303,14 @@
 
 
 def middle_kernel(
+    plan,
     x, part_a, part_b, first, gain, grads, gated_all, gate_all, scan_all, normed_all, weights_all,
-    base_o, scan_grad_o, back_o, pack_o, gain_grad_o,
+    base_o, scan_grad_o, back_o, pack_o, gain_grad_o, begun_o,
     grad, gated, gate, scan_out, normed_a, wq, wk, wv, wm, out_w, w_gate,
     normed, q_t, q_n, k_n, v_n, k_t, v_t, g_n, g_t, o_t, dq_n, dk, dv, bias, expo, prob_grad, prob_low,
     score_low,
     dq_low, dk_low, dv_low, branch, branch_got, back, back_got, base, scan_grad, gate_back, gout, ggate,
-    pack, load_sems, pass_sems, store_sems,
+    pack, land, sum_sems, load_sems, pass_sems, store_sems,
 ):
     length, width = x.shape
     core, row = lax.axis_index("kind"), lax.axis_index("inner")
@@ -333,9 +334,13 @@
     ]
     for load in loads:
         load.start()
+    summing = Summing(plan, pack, None, land, None, None, *sum_sems)
+    digit, _, begun_rows, _ = plan[0][2][0]
     barrier = pltpu.get_barrier_semaphore()
-    pl.semaphore_signal(barrier, inc=1, device_id=other_core, device_id_type=pl.DeviceIdType.MESH)
-    pl.semaphore_wait(barrier, 1)
+    partners = [other_core] + [summing.partner(digit, q) for q in range(1, 1 << len(digit))]
+    for device in partners:
+        pl.semaphore_signal(barrier, inc=1, device_id=device, device_id_type=pl.DeviceIdType.MESH)
+    pl.semaphore_wait(barrier, len(partners))
     for load in loads[:5]:
         load.wait()
 
@@ -441,6 +446,7 @@
     pack[width : width + cut, 0:head_cols] = value_grad[:cut]
     pack[width : width + cut, head_cols:] = value_grad[cut:]
     pack[width + cut : attn_rows, :] = dot_nn(o_t[...], grad[...]).astype(BF16)
+    summing.begin(summing.halves(0, 0))
     for load in loads[5:]:
         load.wait()
     gout[...] = jnp.zeros_like(gout)
@@ -487,6 +493,8 @@
     pack[attn_rows + channels :, :] = ggate[...].astype(BF16)
     last = pltpu.make_async_copy(pack, pack_o, load_sems.at[0])
     last.start()
+    summing.finish(summing.halves(0, 0))
+    summing.add_to(begun_o, 0, 0, 0)
     for b in range(blocks):
         for store in stores(b):
             store.wait()
@@ -598,8 +606,7 @@
 
 
 def conv_back_block(
-    coef_grad, pre, act_grad, conv_in, normed, x, gate_back, flags, state_w, taps, w_conv,
-    ext, gconv, gsmall, taps_at,
+    coef_grad, pre, act_grad, conv_in, normed, flags, state_w, taps, ext, gconv, gsmall, mix_low, taps_at,
 ):
     block = pre.shape[0]
     coefs = coef_grad.shape[0]
@@ -621,20 +628,19 @@
     gsmall[taps_at + 4 : taps_at + 5, :] += jnp.sum(conv_grad, axis=0, keepdims=True)
     low = conv_in_grad.astype(BF16)
     gconv[...] += dot_tn(normed[...], low)
-    back = gate_back[...] + dot_nt(low, w_conv[...])
-    u = x[...].astype(F32)
-    gsmall[taps_at + 5 : taps_at + 6, :] += jnp.sum(back * u * rms_scale(u), axis=0, keepdims=True)
+    mix_low[...] = low
     ext[block:, :] = ext[0:8, :]
-    return back
-
-
-def sum_plan(rows, counts):
+
+
+def sum_digits(counts):
     bits = [(axis, 1 << i) for axis, size in counts for i in range(size.bit_length() - 1)]
-    digits = [bits[i : i + 2] for i in range(0, len(bits), 2)]
-    most = (rows * 13 // 20 + 128) // 256 * 256
-    sizes = [(0, most), (1, rows - most)] if rows > 1024 else [(0, most // 2), (0, most // 2), (1, rows - most)]
+    return [bits[i : i + 2] for i in range(0, len(bits), 2)]
+
+
+def sum_plan(counts, parts):
+    digits = sum_digits(counts)
     streams, at, land = [], 0, 0
-    for number, size in sizes:
+    for number, size, lead in parts:
         turn = number % len(digits)
         steps, held = [], size
         for digit in digits[turn:] + digits[:turn]:
@@ -643,20 +649,21 @@
             held = held // radix if split else held
             steps.append((digit, split, held, land))
             land += held * (radix - 1)
-        streams.append((at, size, steps))
+        streams.append((at, size, steps, lead))
         at += size
     return streams, land
 
 
 class Summing:
-    def __init__(self, plan, src, work, land, full, peer, send, recv):
+    def __init__(self, plan, src, work, land, full, peer, send, recv, given=None):
+        self.given = given
         self.streams, self.src, self.work, self.land = plan, src, work, land
         self.full, self.peer = full, peer
         self.sems = (send, recv)
         self.turns = len(plan[0][2])
-        self.phases = 2 * self.turns + 2
+        self.phases = 2 * self.turns + 2 - min(0, *(lead for _, _, _, lead in plan))
         self.start = []
-        for first, _, steps in plan:
+        for first, _, steps, _ in plan:
             at, spots = first, [first]
             for turn, (digit, split, kept, _) in enumerate(steps):
                 at = at + self.index(digit, 0) * kept if split else at
@@ -708,10 +715,13 @@
         ]
 
     def add(self, s, turn):
+        target = self.full if turn == self.turns - 1 else self.work
+        self.add_to(target, self.start[s][turn + 1], s, turn)
+
+    def add_to(self, target, first, s, turn):
         _, _, kept, land = self.streams[s][2][turn]
         at = self.start[s][turn + 1]
         source = self.src if turn == 0 else self.work
-        target = self.full if turn == self.turns - 1 else self.work
 
         def step(i, unused):
             here = pl.ds(pl.multiple_of(at + i * 16, 16), 16)
@@ -721,7 +731,7 @@
                 parts.append(self.land[there, :].astype(F32))
             while len(parts) > 1:
                 parts = [parts[i] + parts[i + 1] for i in range(0, len(parts), 2)]
-            target[here, :] = parts[0].astype(BF16)
+            target[pl.ds(pl.multiple_of(first + i * 16, 16), 16), :] = parts[0].astype(BF16)
             return unused
 
         lax.fori_loop(0, kept // 16, step, 0)
@@ -750,15 +760,6 @@
             for q, at, size in found
         ]
 
-    def slots(self, count):
-        lengths = [2.5 + 14.0 * 0.5**turn for turn in range(self.turns)]
-        found, at = [0], 0.0
-        for length in lengths + lengths[::-1]:
-            at += length * count / 42.0
-            if at < count - 1:
-                found.append(int(at))
-        return found
-
     def greet(self):
         barrier = pltpu.get_barrier_semaphore()
         partners = [self.other_core()]
@@ -779,26 +780,31 @@
             copy.wait()
 
     def phase(self, number):
-        for s in range(len(self.streams)):
-            if number == 0:
+        for s, (_, _, steps, lead) in enumerate(self.streams):
+            at = number + lead
+            if number == self.phases - 1:
+                for turn in range(self.turns + 1):
+                    self.finish(self.shares(s, turn))
+            elif at == 0:
                 self.begin(self.halves(s, 0))
-            elif number <= self.turns:
-                self.finish(self.halves(s, number - 1))
-                self.add(s, number - 1)
-                if number < self.turns:
-                    self.begin(self.halves(s, number))
+            elif 0 < at <= self.turns:
+                if number == 0:
+                    kept = steps[at - 1][2]
+                    self.work[pl.ds(pl.multiple_of(self.start[s][at], 16), kept), :] = self.given[...]
+                else:
+                    self.finish(self.halves(s, at - 1))
+                    self.add(s, at - 1)
+                if at < self.turns:
+                    self.begin(self.halves(s, at))
                 else:
                     self.begin(self.spreads(s, self.turns - 1))
                     self.begin(self.shares(s, self.turns))
-            elif number <= 2 * self.turns:
-                turn = 2 * self.turns - number
+            elif self.turns < at <= 2 * self.turns:
+                turn = 2 * self.turns - at
                 self.finish(self.spreads(s, turn))
                 if turn > 0:
                     self.begin(self.spreads(s, turn - 1))
                 self.begin(self.shares(s, turn))
-            else:
-                for turn in range(self.turns + 1):
-                    self.finish(self.shares(s, turn))
 
 
 def sum_scratch(plan, rows, land, width):
@@ -824,11 +830,11 @@
 def back_kernel(
     plan, plan_last, steps,
     coef, pre, step_in, scan_grad, flags, starts,
-    pre_late, conv_in, normed, x, gate_back, flags_late,
-    gain, gain_grad, pack, x_all, base_all, weights_all,
+    pre_late, conv_in, normed, flags_late,
+    gain, gain_grad, pack, begun, x_all, base_all, gate_back_all, weights_all,
     early_o, late_o, kept_o, got_o,
     step_w, decay_t, skip, state_w, taps, w_conv, weight_sems,
-    scan_spare, small, act_grads, coef_grads, coef_got, ext, gconv, gsmall, back, low, low_got,
+    scan_spare, small, act_grads, coef_grads, coef_got, ext, gconv, gsmall, mix_low, back, low, low_got,
     x_s, base_s, kept, sent, got, pack_last, sum_spare, sum_spare_last,
     coef_sems, low_sems, pass_sems, local_sems,
 ):
@@ -839,11 +845,12 @@
     taps_at = coefs + small.shape[0]
     core, row = lax.axis_index("kind"), lax.axis_index("inner")
     other_core = {"kind": 1 - core}
-    first_sum = Summing(plan, pack, *sum_spare)
+    first_sum = Summing(plan, pack, *sum_spare, given=begun)
     last_sum = Summing(plan_last, pack_last, *sum_spare_last)
-    slots = first_sum.slots(pairs * steps)
+    slots = [share * pairs * steps // 32 for share in (0, 9, 15, 22, 30)]
     load_x = pltpu.make_async_copy(x_all, x_s, local_sems.at[0])
     load_base = pltpu.make_async_copy(base_all, base_s, local_sems.at[1])
+    load_back = pltpu.make_async_copy(gate_back_all, back, local_sems.at[8])
     mine = pl.ds(pl.multiple_of(core * w_conv.shape[1], 128), w_conv.shape[1])
     load_weights = [
         pltpu.make_async_copy(source.at[:, mine], target, weight_sems.at[i])
@@ -874,6 +881,7 @@
         first_sum.greet()
         load_x.start()
         load_base.start()
+        load_back.start()
         for copy in load_weights:
             copy.wait()
 
@@ -896,13 +904,10 @@
         coef_copy(late).wait()
         coef_low = (coef_grads[late] + coef_got[late]).astype(BF16)
         here = pl.ds(pl.multiple_of((steps - 1 - late) * block, block), block)
-        part = conv_back_block(
-            coef_low, pre_late, act_grads.at[lax.rem(late, 2)], conv_in, normed, x, gate_back,
-            flags_late, state_w, taps, w_conv, ext, gconv, gsmall, taps_at,
+        conv_back_block(
+            coef_low, pre_late, act_grads.at[lax.rem(late, 2)], conv_in, normed, flags_late, state_w,
+            taps, ext, gconv, gsmall, mix_low.at[here], taps_at,
         )
-        back[here, :] = part
-        low[here, :] = part.astype(BF16)
-        low_copy(late).start()
 
     @pl.when(pid == steps)
     def _():
@@ -911,11 +916,27 @@
         gsmall[coefs:taps_at, :] = small[...]
         gsmall[taps_at + 6 : taps_at + 7, :] = gain_grad[...]
         pack_last[0:width, :] = gconv[...].astype(BF16)
-        pack_last[width:, :] = gsmall[...].astype(BF16)
+        pack_last[width : width + 128, :] = gsmall[...].astype(BF16)
         last_sum.phase(0)
+        load_x.wait()
+        load_back.wait()
+        gain_sum = jnp.zeros((1, width), F32)
+        for i in range(steps):
+            here = slice((steps - 1 - i) * block, (steps - i) * block)
+            total = back[here, :] + dot_nt(mix_low[here, :], w_conv[...])
+            back[here, :] = total
+            low[here, :] = total.astype(BF16)
+            low_copy(i).start()
+            u = x_s[here, :].astype(F32)
+            gain_sum += jnp.sum(total * u * rms_scale(u), axis=0, keepdims=True)
+        pack_last[width + 128 :, :] = jnp.concatenate(
+            [gain_sum, jnp.zeros((15, width), F32)], axis=0
+        ).astype(BF16)
+        for number in range(len(slots), first_sum.phases - 1):
+            first_sum.phase(number)
+        last_sum.phase(1)
         for i in range(steps):
             low_copy(i).wait()
-        load_x.wait()
         load_base.wait()
         chosen = (1 - core).astype(F32)
         half = kept.shape[0]
@@ -933,7 +954,7 @@
             lax.fori_loop(0, half // 64, part, 0)
 
         finish((1 - row) * half, sent)
-        pieces = last_sum.phases - 2
+        pieces = 4
         passing = [
             remote(
                 sent.at[pl.ds(i * (half // pieces), half // pieces)],
@@ -944,15 +965,14 @@
         finish(row * half, kept)
         keep = pltpu.make_async_copy(kept, kept_o, local_sems.at[2])
         keep.start()
-        for number in range(len(slots), first_sum.phases):
-            first_sum.phase(number)
+        first_sum.phase(first_sum.phases - 1)
         store_first = both_copies(first_sum, early_o, local_sems, 3)
         for copy in store_first:
             copy.start()
-        for number in range(1, last_sum.phases):
+        for number in range(2, last_sum.phases):
             last_sum.phase(number)
-            if number <= pieces:
-                passing[number - 1].start()
+            if number - 2 < pieces:
+                passing[number - 2].start()
         store_last = both_copies(last_sum, late_o, local_sems, 5)
         for copy in passing:
             copy.wait()
@@ -965,7 +985,7 @@
 
 
 def assemble_kernel(
-    sizes, sel, kept, got, query_key, value, mixed, out, gate, conv, small,
+    sizes, sel, kept, got, query_key, value, mixed, out, gate, conv, small, gains,
     results_o, in_o, out_o, query_o, key_o, value_o, mixed_o,
     state_o, step_o, decay_o, step_bias_o, skip_o, taps_o, conv_bias_o, gain_o, attn_gain_o,
 ):
@@ -995,7 +1015,7 @@
         if target is not None:
             target[...] = both[at : at + size]
         at += size
-    gain_o[...] = both[at : at + 1, :half] + both[at : at + 1, half:]
+    gain_o[...] = gains[0, 0:1].astype(F32) + gains[1, 0:1].astype(F32)
     attn_gain_o[...] = both[at + 1 : at + 2, :half]
 
 
@@ -1138,16 +1158,21 @@
     head_low = pltpu.VMEM((length, head_cols), BF16)
     square = pltpu.VMEM((width, head_cols), BF16)
     pack_rows = width + width // 2 + head_cols + half + width
-    base, scan_grad, gate_back, pack_early, g_attn_gain = pl.pallas_call(
-        middle_kernel,
+    counts = [("inner", lax.axis_size("inner")), ("dp", lax.axis_size("dp"))]
+    attn_rows = width + width // 2 + head_cols
+    plan, land = sum_plan(counts, [(0, attn_rows, 1), (0, pack_rows - attn_rows, 0)])
+    begun_rows = plan[0][2][0][2]
+    base, scan_grad, gate_back, pack_early, g_attn_gain, begun = pl.pallas_call(
+        functools.partial(middle_kernel, plan[:1]),
         in_specs=[vmem_spec] * 5 + [any_spec] * 5 + [(any_spec,) * 6],
-        out_specs=[any_spec] * 4 + [vmem_spec],
+        out_specs=[any_spec] * 4 + [vmem_spec] * 2,
         out_shape=[
             jax.ShapeDtypeStruct((length, width), F32),
             jax.ShapeDtypeStruct((length, half), F32),
             jax.ShapeDtypeStruct((length, width), F32),
             jax.ShapeDtypeStruct((pack_rows, width), BF16),
             jax.ShapeDtypeStruct((1, width), F32),
+            jax.ShapeDtypeStruct((begun_rows, width), BF16),
         ],
         scratch_shapes=[
             tokens_low, pltpu.VMEM((length, half), BF16), pltpu.VMEM((length, half), F32),
@@ -1160,6 +1185,7 @@
             head_low, head_low, head_low, tokens_low, tokens_low, tokens_low, tokens_low, tokens_f32,
             pltpu.VMEM((length, half), F32), tokens_f32, pltpu.VMEM((half, width), F32),
             pltpu.VMEM((width, half), F32), pltpu.VMEM((pack_rows, width), BF16),
+            pltpu.VMEM((3 * begun_rows, width), BF16), pair_of_sems(16),
             pltpu.SemaphoreType.DMA((11,)),
             [pltpu.SemaphoreType.DMA((2 * blocks,)), pltpu.SemaphoreType.DMA((2 * blocks,))],
             pltpu.SemaphoreType.DMA((3, blocks)),
@@ -1174,10 +1200,10 @@
     )(x, branch, branch_other, first, gain_b, output_grad, gated, gate_z, scan_out, normed_a,
       (query_proj, key_proj, value_proj, mixed_proj, out_proj, in_proj))
 
-    counts = [("inner", lax.axis_size("inner")), ("dp", lax.axis_size("dp"))]
-    plan, land = sum_plan(pack_early.shape[0], counts)
-    last_rows = width + 128
-    plan_last, land_last = sum_plan(last_rows, counts)
+    last_rows = width + 144
+    plan_last, land_last = sum_plan(
+        counts, [(0, width // 2, 0), (0, width // 2, 0), (1, 128, 0), (0, 16, -1)]
+    )
     tile_f32 = pltpu.VMEM((2, half // 128, wide, 128), F32)
     tile_low = pltpu.VMEM((2, wide, half), BF16)
     own_f32 = pltpu.VMEM((ROWS_STEP, wide), F32)
@@ -1199,8 +1225,7 @@
         back_rows(scan_grad, now), back_rows(flags, now),
         (starts, (ROWS_STEP // CHUNK * states, half), lambda i: (now(i), 0)),
         back_rows(conv_pre, late_at), back_rows(conv_in, late_at), back_rows(normed_a, late_at),
-        back_rows(x, late_at), back_rows(gate_back, late_at), back_rows(flags, late_at),
-        fixed(gain_a), fixed(g_attn_gain), fixed(pack_early),
+        back_rows(flags, late_at), fixed(gain_a), fixed(g_attn_gain), fixed(pack_early), fixed(begun),
     ]
     weights_all = (step_proj, decay_t, skip, state_t, taps, in_proj)
     specs = [
@@ -1211,7 +1236,7 @@
     early, late, kept, got = pl.pallas_call(
         functools.partial(back_kernel, plan, plan_last, steps),
         grid=(steps + 1,),
-        in_specs=specs + [any_spec] * 2 + [(any_spec,) * len(weights_all)],
+        in_specs=specs + [any_spec] * 3 + [(any_spec,) * len(weights_all)],
         out_specs=[any_spec] * 4,
         out_shape=[
             jax.ShapeDtypeStruct((parts,) + pack_early.shape, BF16),
@@ -1231,6 +1256,7 @@
             pltpu.VMEM((ROWS_STEP + 8, half), F32),
             pltpu.VMEM((width, half), F32),
             pltpu.VMEM((128, half), F32),
+            pltpu.VMEM((length, half), BF16),
             pltpu.VMEM((length, width), F32),
             pltpu.VMEM((length, width), BF16),
             pltpu.VMEM((length, width), BF16),
@@ -1245,7 +1271,7 @@
             [pltpu.SemaphoreType.DMA((steps,)), pltpu.SemaphoreType.DMA((steps,))],
             [pltpu.SemaphoreType.DMA((steps,)), pltpu.SemaphoreType.DMA((steps,))],
             [pltpu.SemaphoreType.DMA((16,)), pltpu.SemaphoreType.DMA((16,))],
-            pltpu.SemaphoreType.DMA((8,)),
+            pltpu.SemaphoreType.DMA((9,)),
         ],
         compiler_params=pltpu.CompilerParams(
             dimension_semantics=("arbitrary",), vmem_limit_bytes=VMEM_BYTES, collective_id=1,
@@ -1255,7 +1281,7 @@
             flops=2 * length * states * half * 3000, bytes_accessed=1 << 25, transcendentals=0
         ),
         name="back",
-    )(*[a for a, _, _ in ins], x, base, weights_all)
+    )(*[a for a, _, _ in ins], x, base, gate_back, weights_all)
     quarter = width // 4
     eighth = width // 8
 
@@ -1265,7 +1291,6 @@
     def out_parts(size):
         return ((parts, 4 * size, width), F32, (parts, size, width), lambda i, sel: (0, i, 0))
 
-    attn_rows = width + width // 2 + head_cols
     results, t_in, t_out, t_query, t_key, t_value, t_mixed, *smalls = call(
         functools.partial(assemble_kernel, (coefs, rank, states)), sel, 4,
         [(kept, (piece_len // 4, width), lambda i, sel: (i, 0)),
@@ -1273,7 +1298,8 @@
          from_sum(early, quarter, 0), from_sum(early, eighth, width),
          from_sum(early, eighth, width + width // 2), from_sum(early, quarter, attn_rows),
          from_sum(early, quarter, attn_rows + half), from_sum(late, quarter, 0),
-         (late, (parts, 128, width), lambda i, sel: (0, width // 128, 0))],
+         (late, (parts, 128, width), lambda i, sel: (0, width // 128, 0)),
+         (late, (parts, 16, width), lambda i, sel: (0, (width + 128) // 16, 0))],
         [((1, 2, piece_len, width), F32, (1, 2, piece_len // 4, width), lambda i, sel: (0, 0, i, 0)),
          ((width, 4 * half), F32, (quarter, 4 * half), lambda i, sel: (i, 0)),
          out_parts(quarter), ((width, width), F32, (quarter, width), lambda i, sel: (i, 0)),

time: 178 us -> 183 us (1.028)
  Pallas kernels: 174 us -> 180 us
    pallas_call x1, Pallas kernels: 34 us -> 41.5 us  [local(): pl.pallas_call(functools.partial(middle_kernel, plan[:1]), in_specs=[vmem...]
where the time goes in v1:
time: 183 us
  Pallas kernels  180 us (98%)
  other arithmetic  2.07 us (1%)
    pallas_call x1, Pallas kernels, local(): pl.pallas_call(functools.partial(back_kernel, plan, plan_last, steps), gr...  92.8 us
    pallas_call x1, Pallas kernels, local(): pl.pallas_call(functools.partial(middle_kernel, plan[:1]), in_specs=[vmem...  41.5 us
    pallas_call x1, Pallas kernels, local(): pl.pallas_call(front_kernel, in_specs=[pl.BlockSpec(memory_space=pltpu.VM...  36.1 us
    pallas_call x1, Pallas kernels, call(): pl.pallas_call(body, grid_spec=pltpu.PrefetchScalarGridSpec(num_scalar_pr...  9.23 us

profile of v1, /device:TPU:0, one launch (start us, length us, event | category | flops | bytes accessed | tf_op | source)
XLA Modules:
  0.0 183.2 jit_solution(2283312418179912478)
XLA Ops:
  0.6 0.0 copy-start
  0.7 0.6 pad_add_fusion.sel
  1.2 0.1 copy-done
  1.4 0.6 convert_reduce_fusion
  1.9 0.0 copy-start.1
  1.9 0.1 fusion.2
  2.1 0.1 stack.32
  2.2 0.3 copy.39
  2.4 0.8 convert_element_type.7.flags.flags_late
  3.3 36.1 %front.1 = (bf16[1024,512]{1,0:T(8,128)(2,1)}, bf16[1024,512]{1,0:T(8,128)(2,1)}, f32[1024,512]{1,0:T(8,128)}, f32[1024,512]{1,0:T(8,128)}, f32[1024,512]{1,0:T(...) custom-call(f32[1024,8]{1,0:T(8,128)} %convert_element_type.7.flags., ...), custom_call_target="tpu_custom_call" | custom-call | flops 16777216000 | bytes 16777216 | tf_op jit(solution)/shard_map/front/pallas_call | solution.py:1117
  39.4 0.0 copy-done.1
  39.4 41.5 %middle.1 = (f32[1024,512]{1,0:T(8,128)}, f32[1024,512]{1,0:T(8,128)}, f32[1024,512]{1,0:T(8,128)}, bf16[2048,512]{1,0:T(8,128)(2,1)}, f32[1,512]{1,0:T(1,128)}, /*index=5*/bf16[256,512]{1,0:T(8,128)(2,1)}) custom-call(bf16[1024,512]{1,0:T(8,128)(2,1)} %get-tuple-element.57.x.x_all, bf16[1024,512]{1,0:T(8,128)(2,1)} %get-tuple-element.58.part_a, ...), custom_call_target="tpu_custom_call" | custom-call | flops 10737418240 | bytes 16777216 | tf_op jit(solution)/shard_map/middle/pallas_call | solution.py:1165
  80.9 92.8 %back.1 = (bf16[2,2048,512]{2,1,0:T(8,128)(2,1)}, bf16[2,656,512]{2,1,0:T(8,128)(2,1)}, f32[512,512]{1,0:T(8,128)}, bf16[512,512]{1,0:T(8,128)(2,1)}) custom-call(f32[4,64,256]{2,1,0:T(8,128)} %get-tuple-element.54.coef, f32[1024,512]{1,0:T(8,128)} %get-tuple-element.55.pre.pre_late, f32[1024,512]{1,0:T(8,128)} %get-tuple-element.56.step_in, ...), custom_call_target="tpu_custom_call" | custom-call | flops 50331648000 | bytes 33554432 | tf_op jit(solution)/shard_map/back/pallas_call | solution.py:1236
  173.7 9.2 %assemble.1 = (f32[1,2,512,512]{3,2,1,0:T(8,128)}, f32[512,2048]{1,0:T(8,128)}, f32[2,512,512]{2,1,0:T(8,128)}, f32[512,512]{1,0:T(8,128)}, f32[512,512]{1,0:T(8...) custom-call(s32[2]{0:T(128)} %pad_add_fusion.sel, ...), custom_call_target="tpu_custom_call" | custom-call | bytes 26574848 | tf_op jit(solution)/shard_map/assemble/pallas_call | solution.py:90
  (6 shorter events, 0.1 us)
Async XLA Ops:
  0.6 0.7 copy-start
  1.9 37.5 %copy-start.1 = (s32[1024]{0:T(1024)}, s32[1024]{0:T(1024)S(1)}, u32[]{:S(2)}) copy-start(s32[1024]{0:T(1024)S(1)} %convert_reduce_fusion) | copy-start | bytes 12292

commit v2 on v1

--- a/solution.py
+++ b/solution.py
@@ -303,14 +303,13 @@
 
 
 def middle_kernel(
-    plan,
     x, part_a, part_b, first, gain, grads, gated_all, gate_all, scan_all, normed_all, weights_all,
-    base_o, scan_grad_o, back_o, pack_o, gain_grad_o, begun_o,
+    base_o, scan_grad_o, back_o, pack_o, gain_grad_o,
     grad, gated, gate, scan_out, normed_a, wq, wk, wv, wm, out_w, w_gate,
     normed, q_t, q_n, k_n, v_n, k_t, v_t, g_n, g_t, o_t, dq_n, dk, dv, bias, expo, prob_grad, prob_low,
     score_low,
     dq_low, dk_low, dv_low, branch, branch_got, back, back_got, base, scan_grad, gate_back, gout, ggate,
-    pack, land, sum_sems, load_sems, pass_sems, store_sems,
+    pack, load_sems, pass_sems, store_sems,
 ):
     length, width = x.shape
     core, row = lax.axis_index("kind"), lax.axis_index("inner")
@@ -334,13 +333,9 @@
     ]
     for load in loads:
         load.start()
-    summing = Summing(plan, pack, None, land, None, None, *sum_sems)
-    digit, _, begun_rows, _ = plan[0][2][0]
     barrier = pltpu.get_barrier_semaphore()
-    partners = [other_core] + [summing.partner(digit, q) for q in range(1, 1 << len(digit))]
-    for device in partners:
-        pl.semaphore_signal(barrier, inc=1, device_id=device, device_id_type=pl.DeviceIdType.MESH)
-    pl.semaphore_wait(barrier, len(partners))
+    pl.semaphore_signal(barrier, inc=1, device_id=other_core, device_id_type=pl.DeviceIdType.MESH)
+    pl.semaphore_wait(barrier, 1)
     for load in loads[:5]:
         load.wait()
 
@@ -446,7 +441,6 @@
     pack[width : width + cut, 0:head_cols] = value_grad[:cut]
     pack[width : width + cut, head_cols:] = value_grad[cut:]
     pack[width + cut : attn_rows, :] = dot_nn(o_t[...], grad[...]).astype(BF16)
-    summing.begin(summing.halves(0, 0))
     for load in loads[5:]:
         load.wait()
     gout[...] = jnp.zeros_like(gout)
@@ -493,8 +487,6 @@
     pack[attn_rows + channels :, :] = ggate[...].astype(BF16)
     last = pltpu.make_async_copy(pack, pack_o, load_sems.at[0])
     last.start()
-    summing.finish(summing.halves(0, 0))
-    summing.add_to(begun_o, 0, 0, 0)
     for b in range(blocks):
         for store in stores(b):
             store.wait()
@@ -505,8 +497,7 @@
     coef, pre, step_in, scan_grad, flags, starts, step_w, decay_t, skip,
     act_grad, coef_grad, small, spare, between,
 ):
-    (state, steps, stepd, drive, reads, blocked, d_drive, d_expo, in_own, read_own,
-     decays, decayed, h_low, sum_low, expo_low) = spare
+    state, steps, stepd, drive, reads, blocked, d_drive, d_expo, *pair_spare = spare
     block, width = pre.shape
     states = decay_t.shape[0]
     rank = step_w.shape[0]
@@ -525,13 +516,15 @@
     picks = state_picks(CHUNK, states)
     own = own_token(CHUNK, states)
     own_low = own.astype(F32).astype(BF16)
+    ones = jnp.ones((128, 128), BF16)
+    coef_grad[rank:, :] = jnp.zeros((2 * states, block), F32)
     own_all = jnp.concatenate([own] * (block // CHUNK), axis=0)
     blocked[...] = jnp.where(
         own_all, dot_tn(coef[rank : rank + states, :].astype(BF16), picks), 0.0
     ).astype(BF16)
 
     def one_chunk(i, backward, spare):
-        decay_s, decayed_s, h_s, sum_s, expo_s = spare
+        decay_s, decayed_s, sum_s, expo_s, in_s, read_s = spare
         rows16 = pl.ds(pl.multiple_of(i * CHUNK, CHUNK), CHUNK)
         tile = coef[rank:, pl.ds(pl.multiple_of((i // 8) * 128, 128), 128)]
         tile = pltpu.roll(tile, lax.rem(128 - lax.rem(i, 8) * CHUNK, 128), 1)
@@ -544,10 +537,12 @@
                 cols = slice(c * 128, (c + 1) * 128)
                 decay = jnp.exp(neg_of[c] * row_of(stepd, c, row, states))
                 kept = decay * h[c]
+                decay_s[c, here, :] = decay
                 h[c] = kept + row_of(drive, c, row, states) * write
-                decay_s[c, here, :] = decay
                 decayed_s[c, here, :] = kept
-                h_s[here, cols] = h[c].astype(BF16)
+                part = h[c] * row_of(reads, c, row, states)
+                reading = part if c == 0 else reading + part
+            read_s[here, :] = reading.astype(BF16)
         total = [jnp.zeros((states, 128), F32)] * tiles
         for at in reversed(range(CHUNK)):
             row = i * CHUNK + at
@@ -561,16 +556,22 @@
                 expo_s[here, cols] = (expo * neg_of[c]).astype(BF16)
                 total[c] = total[c] + expo * row_of(steps, c, row, states)
                 backward[c] = decay_s[c, here, :] * summed
+                part = summed * row_of(drive, c, row, states)
+                writing = part if c == 0 else writing + part
+            in_s[here, :] = writing.astype(BF16)
         for c in range(tiles):
             small[rank : rank + states, c * 128 : (c + 1) * 128] += total[c]
 
-        def flat(ref):
-            return jnp.concatenate([ref[c, rows16, :] for c in range(tiles)], axis=1).astype(BF16)
-
         d_drive[rows16, :] = dot_nn(blocked[rows16, :], sum_s[...])
         d_expo[rows16, :] = dot_nn(own_low, expo_s[...])
-        in_own[rows16, :] = jnp.where(own, dot_nt(flat(drive), sum_s[...]), 0.0)
-        read_own[rows16, :] = jnp.where(own, dot_nt(flat(reads), h_s[...]), 0.0)
+        lanes = pl.ds(pl.multiple_of((i // 8) * 128, 128), 128)
+        own_lane = lax.broadcasted_iota(jnp.int32, (states, 128), 1) - lax.rem(i, 8) * CHUNK
+        for low_s, at_row in ((in_s, rank), (read_s, rank + states)):
+            lane_sums = dot_nn(low_s[...], ones)
+            placed = jnp.zeros((states, 128), F32)
+            for at in range(CHUNK):
+                placed = jnp.where(own_lane == at, lane_sums[at * states : (at + 1) * states, :], placed)
+            coef_grad[at_row : at_row + states, lanes] += placed
         return backward
 
     def pair(step_no, carried):
@@ -578,21 +579,12 @@
         backward = list(carried)
         last = block // CHUNK - 1 - 2 * step_no
         for sub in range(2):
-            spare = (decays.at[sub], decayed.at[sub], h_low.at[sub], sum_low.at[sub], expo_low.at[sub])
-            backward = one_chunk(last - sub, backward, spare)
+            backward = one_chunk(last - sub, backward, pair_spare[sub])
         return tuple(backward)
 
     begin = tuple(state[:, c * 128 : (c + 1) * 128] for c in range(tiles))
     for c, last in enumerate(lax.fori_loop(0, block // (2 * CHUNK), pair, begin)):
         state[:, c * 128 : (c + 1) * 128] = last
-
-    def by_state(ref):
-        high = ref[...].astype(BF16)
-        rest = (ref[...] - high.astype(F32)).astype(BF16)
-        return dot_nt(picks, high) + dot_nt(picks, rest)
-
-    coef_grad[rank : rank + states, :] = by_state(in_own)
-    coef_grad[rank + states :, :] = by_state(read_own)
 
     drive_grad = d_drive[...]
     pre_grad = (d_expo[...] + drive_grad * act) * jax.nn.sigmoid(step_pre)
@@ -655,8 +647,7 @@
 
 
 class Summing:
-    def __init__(self, plan, src, work, land, full, peer, send, recv, given=None):
-        self.given = given
+    def __init__(self, plan, src, work, land, full, peer, send, recv):
         self.streams, self.src, self.work, self.land = plan, src, work, land
         self.full, self.peer = full, peer
         self.sems = (send, recv)
@@ -780,7 +771,7 @@
             copy.wait()
 
     def phase(self, number):
-        for s, (_, _, steps, lead) in enumerate(self.streams):
+        for s, (_, _, _, lead) in enumerate(self.streams):
             at = number + lead
             if number == self.phases - 1:
                 for turn in range(self.turns + 1):
@@ -788,12 +779,8 @@
             elif at == 0:
                 self.begin(self.halves(s, 0))
             elif 0 < at <= self.turns:
-                if number == 0:
-                    kept = steps[at - 1][2]
-                    self.work[pl.ds(pl.multiple_of(self.start[s][at], 16), kept), :] = self.given[...]
-                else:
-                    self.finish(self.halves(s, at - 1))
-                    self.add(s, at - 1)
+                self.finish(self.halves(s, at - 1))
+                self.add(s, at - 1)
                 if at < self.turns:
                     self.begin(self.halves(s, at))
                 else:
@@ -831,7 +818,7 @@
     plan, plan_last, steps,
     coef, pre, step_in, scan_grad, flags, starts,
     pre_late, conv_in, normed, flags_late,
-    gain, gain_grad, pack, begun, x_all, base_all, gate_back_all, weights_all,
+    gain, gain_grad, pack, x_all, base_all, gate_back_all, weights_all,
     early_o, late_o, kept_o, got_o,
     step_w, decay_t, skip, state_w, taps, w_conv, weight_sems,
     scan_spare, small, act_grads, coef_grads, coef_got, ext, gconv, gsmall, mix_low, back, low, low_got,
@@ -845,9 +832,9 @@
     taps_at = coefs + small.shape[0]
     core, row = lax.axis_index("kind"), lax.axis_index("inner")
     other_core = {"kind": 1 - core}
-    first_sum = Summing(plan, pack, *sum_spare, given=begun)
+    first_sum = Summing(plan, pack, *sum_spare)
     last_sum = Summing(plan_last, pack_last, *sum_spare_last)
-    slots = [share * pairs * steps // 32 for share in (0, 9, 15, 22, 30)]
+    slots = [share * pairs * steps // 32 for share in (0, 13, 20, 28)]
     load_x = pltpu.make_async_copy(x_all, x_s, local_sems.at[0])
     load_base = pltpu.make_async_copy(base_all, base_s, local_sems.at[1])
     load_back = pltpu.make_async_copy(gate_back_all, back, local_sems.at[8])
@@ -1160,19 +1147,18 @@
     pack_rows = width + width // 2 + head_cols + half + width
     counts = [("inner", lax.axis_size("inner")), ("dp", lax.axis_size("dp"))]
     attn_rows = width + width // 2 + head_cols
-    plan, land = sum_plan(counts, [(0, attn_rows, 1), (0, pack_rows - attn_rows, 0)])
-    begun_rows = plan[0][2][0][2]
-    base, scan_grad, gate_back, pack_early, g_attn_gain, begun = pl.pallas_call(
-        functools.partial(middle_kernel, plan[:1]),
+    most = (pack_rows * 13 // 20 + 128) // 256 * 256
+    plan, land = sum_plan(counts, [(0, most, 0), (1, pack_rows - most, 0)])
+    base, scan_grad, gate_back, pack_early, g_attn_gain = pl.pallas_call(
+        middle_kernel,
         in_specs=[vmem_spec] * 5 + [any_spec] * 5 + [(any_spec,) * 6],
-        out_specs=[any_spec] * 4 + [vmem_spec] * 2,
+        out_specs=[any_spec] * 4 + [vmem_spec],
         out_shape=[
             jax.ShapeDtypeStruct((length, width), F32),
             jax.ShapeDtypeStruct((length, half), F32),
             jax.ShapeDtypeStruct((length, width), F32),
             jax.ShapeDtypeStruct((pack_rows, width), BF16),
             jax.ShapeDtypeStruct((1, width), F32),
-            jax.ShapeDtypeStruct((begun_rows, width), BF16),
         ],
         scratch_shapes=[
             tokens_low, pltpu.VMEM((length, half), BF16), pltpu.VMEM((length, half), F32),
@@ -1185,7 +1171,6 @@
             head_low, head_low, head_low, tokens_low, tokens_low, tokens_low, tokens_low, tokens_f32,
             pltpu.VMEM((length, half), F32), tokens_f32, pltpu.VMEM((half, width), F32),
             pltpu.VMEM((width, half), F32), pltpu.VMEM((pack_rows, width), BF16),
-            pltpu.VMEM((3 * begun_rows, width), BF16), pair_of_sems(16),
             pltpu.SemaphoreType.DMA((11,)),
             [pltpu.SemaphoreType.DMA((2 * blocks,)), pltpu.SemaphoreType.DMA((2 * blocks,))],
             pltpu.SemaphoreType.DMA((3, blocks)),
@@ -1204,9 +1189,10 @@
     plan_last, land_last = sum_plan(
         counts, [(0, width // 2, 0), (0, width // 2, 0), (1, 128, 0), (0, 16, -1)]
     )
-    tile_f32 = pltpu.VMEM((2, half // 128, wide, 128), F32)
-    tile_low = pltpu.VMEM((2, wide, half), BF16)
-    own_f32 = pltpu.VMEM((ROWS_STEP, wide), F32)
+    tile_f32 = pltpu.VMEM((half // 128, wide, 128), F32)
+    tile_low = pltpu.VMEM((wide, half), BF16)
+    fold_low = pltpu.VMEM((wide, 128), BF16)
+    chunk_spare = [tile_f32, tile_f32, tile_low, tile_low, fold_low, fold_low]
 
     def now(i):
         return jnp.maximum(steps - 1 - i, 0)
@@ -1225,7 +1211,7 @@
         back_rows(scan_grad, now), back_rows(flags, now),
         (starts, (ROWS_STEP // CHUNK * states, half), lambda i: (now(i), 0)),
         back_rows(conv_pre, late_at), back_rows(conv_in, late_at), back_rows(normed_a, late_at),
-        back_rows(flags, late_at), fixed(gain_a), fixed(g_attn_gain), fixed(pack_early), fixed(begun),
+        back_rows(flags, late_at), fixed(gain_a), fixed(g_attn_gain), fixed(pack_early),
     ]
     weights_all = (step_proj, decay_t, skip, state_t, taps, in_proj)
     specs = [
@@ -1248,7 +1234,7 @@
             pltpu.SemaphoreType.DMA((len(weights_all),)),
             [pltpu.VMEM((states, half), F32), block_f32,
              block_f32, block_f32, block_f32, pltpu.VMEM((ROWS_STEP, wide), BF16), plain_f32,
-             plain_f32, own_f32, own_f32, tile_f32, tile_f32, tile_low, tile_low, tile_low],
+             plain_f32, chunk_spare, chunk_spare],
             pltpu.VMEM((small_rows, half), F32),
             pltpu.VMEM((2, ROWS_STEP, half), F32),
             pltpu.VMEM((steps, coefs, ROWS_STEP), F32),

time: 183 us -> 181 us (0.989)
  Pallas kernels: 180 us -> 177 us
    pallas_call x1, Pallas kernels: 41.5 us -> 34 us  [local(): pl.pallas_call(middle_kernel, in_specs=[vmem_spec] * 5 + [any_spec] * 5 +...]
    pallas_call x1, Pallas kernels: 92.8 us -> 97.8 us  [local(): pl.pallas_call(functools.partial(back_kernel, plan, plan_last, steps), gr...]
where the time goes in v2:
time: 181 us
  Pallas kernels  177 us (98%)
  other arithmetic  2.07 us (1%)
    pallas_call x1, Pallas kernels, local(): pl.pallas_call(functools.partial(back_kernel, plan, plan_last, steps), gr...  97.8 us
    pallas_call x1, Pallas kernels, local(): pl.pallas_call(front_kernel, in_specs=[pl.BlockSpec(memory_space=pltpu.VM...  36.2 us
    pallas_call x1, Pallas kernels, local(): pl.pallas_call(middle_kernel, in_specs=[vmem_spec] * 5 + [any_spec] * 5 +...  34 us
    pallas_call x1, Pallas kernels, call(): pl.pallas_call(body, grid_spec=pltpu.PrefetchScalarGridSpec(num_scalar_pr...  9.23 us

profile of v2, /device:TPU:0, one launch (start us, length us, event | category | flops | bytes accessed | tf_op | source)
XLA Modules:
  0.0 180.7 jit_solution(16675885324249190436)
XLA Ops:
  0.6 0.0 copy-start
  0.7 0.6 pad_add_fusion.sel
  1.2 0.1 copy-done
  1.4 0.6 convert_reduce_fusion
  1.9 0.0 copy-start.1
  1.9 0.1 fusion.2
  2.1 0.1 stack.32
  2.2 0.3 copy.39
  2.4 0.8 convert_element_type.7.flags.flags_late
  3.3 36.2 %front.1 = (bf16[1024,512]{1,0:T(8,128)(2,1)}, bf16[1024,512]{1,0:T(8,128)(2,1)}, f32[1024,512]{1,0:T(8,128)}, f32[1024,512]{1,0:T(8,128)}, f32[1024,512]{1,0:T(...) custom-call(f32[1024,8]{1,0:T(8,128)} %convert_element_type.7.flags., ...), custom_call_target="tpu_custom_call" | custom-call | flops 16777216000 | bytes 16777216 | tf_op jit(solution)/shard_map/front/pallas_call | solution.py:1104
  39.4 0.0 copy-done.1
  39.5 34.0 %middle.1 = (f32[1024,512]{1,0:T(8,128)}, f32[1024,512]{1,0:T(8,128)}, f32[1024,512]{1,0:T(8,128)}, bf16[2048,512]{1,0:T(8,128)(2,1)}, f32[1,512]{1,0:T(1,128)}) custom-call(bf16[1024,512]{1,0:T(8,128)(2,1)} %get-tuple-element.56.x.x_all, bf16[1024,512]{1,0:T(8,128)(2,1)} %get-tuple-element.57.part_a, bf16[1024,512]{1,0:T(8,128)(2,1)} %get-tuple-element.58.part_b, ...), custom_call_target="tpu_custom_call" | custom-call | flops 10737418240 | bytes 16777216 | tf_op jit(solution)/shard_map/middle/pallas_call | solution.py:1152
  73.4 97.8 %back.1 = (bf16[2,2048,512]{2,1,0:T(8,128)(2,1)}, bf16[2,656,512]{2,1,0:T(8,128)(2,1)}, f32[512,512]{1,0:T(8,128)}, bf16[512,512]{1,0:T(8,128)(2,1)}) custom-call(f32[4,64,256]{2,1,0:T(8,128)} %get-tuple-element.53.coef, f32[1024,512]{1,0:T(8,128)} %get-tuple-element.54.pre.pre_late, f32[1024,512]{1,0:T(8,128)} %get-tuple-element.55.step_in, ...), custom_call_target="tpu_custom_call" | custom-call | flops 50331648000 | bytes 33554432 | tf_op jit(solution)/shard_map/back/pallas_call | solution.py:1222
  171.3 9.2 %assemble.1 = (f32[1,2,512,512]{3,2,1,0:T(8,128)}, f32[512,2048]{1,0:T(8,128)}, f32[2,512,512]{2,1,0:T(8,128)}, f32[512,512]{1,0:T(8,128)}, f32[512,512]{1,0:T(8...) custom-call(s32[2]{0:T(128)} %pad_add_fusion.sel, ...), custom_call_target="tpu_custom_call" | custom-call | bytes 26574848 | tf_op jit(solution)/shard_map/assemble/pallas_call | solution.py:90
  (6 shorter events, 0.1 us)
Async XLA Ops:
  0.6 0.7 copy-start
  1.9 37.5 %copy-start.1 = (s32[1024]{0:T(1024)}, s32[1024]{0:T(1024)S(1)}, u32[]{:S(2)}) copy-start(s32[1024]{0:T(1024)S(1)} %convert_reduce_fusion) | copy-start | bytes 12292

commit v3 on v2

--- a/solution.py
+++ b/solution.py
@@ -112,7 +112,7 @@
 
 def scan_block(
     coef, pre, gate, flags, step_w, step_b, decay_t, skip, out_w,
-    step_o, scan_o, gated_o, starts_o, branch_o, spare,
+    step_o, size_o, act_o, scan_o, gated_o, starts_o, branch_o, spare,
 ):
     state, stepd, drive, ys, blocked, h_low = spare
     block, width = pre.shape
@@ -123,7 +123,9 @@
     step_pre = dot_tn(coef[:rank, :].astype(BF16), step_w[...]) + step_b[...]
     step_o[...] = step_pre
     step = softplus(step_pre)
+    size_o[...] = step
     act = pre[...] * jax.nn.sigmoid(pre[...])
+    act_o[...] = act
     spread(drive, step * act)
     spread(stepd, jnp.where(flags[:, 1:2] > 0.0, step, FAR))
     neg = -jnp.exp(decay_t[...])
@@ -177,9 +179,10 @@
 
 def front_kernel(
     flags, gain, layer_all, weights_all,
-    x_o, normed_o, conv_o, pre_o, gate_o, coef_o, step_o, scan_o, gated_o, starts_o, branch_o, branch_other_o,
-    x, normed, ext, pre, gate, coef, coef_got, coef_sum, step_pre, scan_out, gated, starts, branch,
-    branch_got, weights, scan_spare, load_sems, x_sems, coef_sems, branch_sems, store_sems, late_sems,
+    x_o, normed_o, conv_o, pre_o, gate_o, coef_o, step_o, size_o, act_o, scan_o, gated_o, starts_o, branch_o,
+    branch_other_o,
+    x, normed, ext, pre, gate, coef, coef_got, coef_sum, step_pre, size, act, scan_out, gated, starts,
+    branch, branch_got, weights, scan_spare, load_sems, x_sems, coef_sems, branch_sems, store_sems, late_sems,
 ):
     length, width = x.shape
     blocks = length // ROWS_STEP
@@ -222,8 +225,8 @@
     scan_spare[0][...] = jnp.zeros_like(scan_spare[0])
 
     results = (
-        (x, x_o), (normed, normed_o), (gate, gate_o), (pre, pre_o), (step_pre, step_o),
-        (scan_out, scan_o), (gated, gated_o), (starts, starts_o), (branch, branch_o),
+        (x, x_o), (normed, normed_o), (gate, gate_o), (pre, pre_o), (step_pre, step_o), (size, size_o),
+        (act, act_o), (scan_out, scan_o), (gated, gated_o), (starts, starts_o), (branch, branch_o),
     )
 
     def stores(b, numbers=range(len(results))):
@@ -280,7 +283,7 @@
         coef_sum[b] = coef[b] + coef_got[b]
         scan_block(
             coef_sum.at[b], pre.at[rows], gate.at[rows], flags.at[rows], step_w, step_b, decay_t, skip, out_w,
-            step_pre.at[rows], scan_out.at[rows], gated.at[rows], starts.at[rows], branch.at[rows],
+            step_pre.at[rows], size.at[rows], act.at[rows], scan_out.at[rows], gated.at[rows], starts.at[rows], branch.at[rows],
             scan_spare,
         )
         branch_copy(b).start()
@@ -494,19 +497,18 @@
 
 
 def scan_back_block(
-    coef, pre, step_in, scan_grad, flags, starts, step_w, decay_t, skip,
+    coef, act_in, size_in, step_in, scan_grad, flags, starts, step_w, decay_t, skip,
     act_grad, coef_grad, small, spare, between,
 ):
-    state, steps, stepd, drive, reads, blocked, d_drive, d_expo, *pair_spare = spare
-    block, width = pre.shape
+    (state, steps, stepd, drive, reads, blocked, d_drive, d_expo, in_own, read_own,
+     decays, decayed, h_low, sum_low, expo_low) = spare
+    block, width = act_in.shape
     states = decay_t.shape[0]
     rank = step_w.shape[0]
     tiles = width // 128
     wide = CHUNK * states
 
-    step_pre = step_in[...]
-    step = softplus(step_pre)
-    act = pre[...] * jax.nn.sigmoid(pre[...])
+    step, act = size_in[...], act_in[...]
     spread(steps, step)
     spread(drive, step * act)
     spread(stepd, jnp.where(flags[:, 1:2] > 0.0, step, FAR))
@@ -516,15 +518,13 @@
     picks = state_picks(CHUNK, states)
     own = own_token(CHUNK, states)
     own_low = own.astype(F32).astype(BF16)
-    ones = jnp.ones((128, 128), BF16)
-    coef_grad[rank:, :] = jnp.zeros((2 * states, block), F32)
     own_all = jnp.concatenate([own] * (block // CHUNK), axis=0)
     blocked[...] = jnp.where(
         own_all, dot_tn(coef[rank : rank + states, :].astype(BF16), picks), 0.0
     ).astype(BF16)
 
     def one_chunk(i, backward, spare):
-        decay_s, decayed_s, sum_s, expo_s, in_s, read_s = spare
+        decay_s, decayed_s, h_s, sum_s, expo_s = spare
         rows16 = pl.ds(pl.multiple_of(i * CHUNK, CHUNK), CHUNK)
         tile = coef[rank:, pl.ds(pl.multiple_of((i // 8) * 128, 128), 128)]
         tile = pltpu.roll(tile, lax.rem(128 - lax.rem(i, 8) * CHUNK, 128), 1)
@@ -537,12 +537,10 @@
                 cols = slice(c * 128, (c + 1) * 128)
                 decay = jnp.exp(neg_of[c] * row_of(stepd, c, row, states))
                 kept = decay * h[c]
+                h[c] = kept + row_of(drive, c, row, states) * write
                 decay_s[c, here, :] = decay
-                h[c] = kept + row_of(drive, c, row, states) * write
                 decayed_s[c, here, :] = kept
-                part = h[c] * row_of(reads, c, row, states)
-                reading = part if c == 0 else reading + part
-            read_s[here, :] = reading.astype(BF16)
+                h_s[here, cols] = h[c].astype(BF16)
         total = [jnp.zeros((states, 128), F32)] * tiles
         for at in reversed(range(CHUNK)):
             row = i * CHUNK + at
@@ -556,22 +554,16 @@
                 expo_s[here, cols] = (expo * neg_of[c]).astype(BF16)
                 total[c] = total[c] + expo * row_of(steps, c, row, states)
                 backward[c] = decay_s[c, here, :] * summed
-                part = summed * row_of(drive, c, row, states)
-                writing = part if c == 0 else writing + part
-            in_s[here, :] = writing.astype(BF16)
         for c in range(tiles):
             small[rank : rank + states, c * 128 : (c + 1) * 128] += total[c]
 
+        def flat(ref):
+            return jnp.concatenate([ref[c, rows16, :] for c in range(tiles)], axis=1).astype(BF16)
+
         d_drive[rows16, :] = dot_nn(blocked[rows16, :], sum_s[...])
         d_expo[rows16, :] = dot_nn(own_low, expo_s[...])
-        lanes = pl.ds(pl.multiple_of((i // 8) * 128, 128), 128)
-        own_lane = lax.broadcasted_iota(jnp.int32, (states, 128), 1) - lax.rem(i, 8) * CHUNK
-        for low_s, at_row in ((in_s, rank), (read_s, rank + states)):
-            lane_sums = dot_nn(low_s[...], ones)
-            placed = jnp.zeros((states, 128), F32)
-            for at in range(CHUNK):
-                placed = jnp.where(own_lane == at, lane_sums[at * states : (at + 1) * states, :], placed)
-            coef_grad[at_row : at_row + states, lanes] += placed
+        in_own[rows16, :] = jnp.where(own, dot_nt(flat(drive), sum_s[...]), 0.0)
+        read_own[rows16, :] = jnp.where(own, dot_nt(flat(reads), h_s[...]), 0.0)
         return backward
 
     def pair(step_no, carried):
@@ -579,15 +571,24 @@
         backward = list(carried)
         last = block // CHUNK - 1 - 2 * step_no
         for sub in range(2):
-            backward = one_chunk(last - sub, backward, pair_spare[sub])
+            spare = (decays.at[sub], decayed.at[sub], h_low.at[sub], sum_low.at[sub], expo_low.at[sub])
+            backward = one_chunk(last - sub, backward, spare)
         return tuple(backward)
 
     begin = tuple(state[:, c * 128 : (c + 1) * 128] for c in range(tiles))
     for c, last in enumerate(lax.fori_loop(0, block // (2 * CHUNK), pair, begin)):
         state[:, c * 128 : (c + 1) * 128] = last
 
+    def by_state(ref):
+        high = ref[...].astype(BF16)
+        rest = (ref[...] - high.astype(F32)).astype(BF16)
+        return dot_nt(picks, high) + dot_nt(picks, rest)
+
+    coef_grad[rank : rank + states, :] = by_state(in_own)
+    coef_grad[rank + states :, :] = by_state(read_own)
+
     drive_grad = d_drive[...]
-    pre_grad = (d_expo[...] + drive_grad * act) * jax.nn.sigmoid(step_pre)
+    pre_grad = (d_expo[...] + drive_grad * act) * jax.nn.sigmoid(step_in[...])
     tail = rank + states
     small[tail : tail + 1, :] += jnp.sum(pre_grad, axis=0, keepdims=True)
     pre_low = pre_grad.astype(BF16)
@@ -816,7 +817,7 @@
 
 def back_kernel(
     plan, plan_last, steps,
-    coef, pre, step_in, scan_grad, flags, starts,
+    coef, act_in, size_in, step_in, scan_grad, flags, starts,
     pre_late, conv_in, normed, flags_late,
     gain, gain_grad, pack, x_all, base_all, gate_back_all, weights_all,
     early_o, late_o, kept_o, got_o,
@@ -827,14 +828,14 @@
 ):
     pid = pl.program_id(0)
     states, rank, coefs = decay_t.shape[0], step_w.shape[0], state_w.shape[0]
-    block = pre.shape[0]
+    block = act_in.shape[0]
     pairs = block // (2 * CHUNK)
     taps_at = coefs + small.shape[0]
     core, row = lax.axis_index("kind"), lax.axis_index("inner")
     other_core = {"kind": 1 - core}
     first_sum = Summing(plan, pack, *sum_spare)
     last_sum = Summing(plan_last, pack_last, *sum_spare_last)
-    slots = [share * pairs * steps // 32 for share in (0, 13, 20, 28)]
+    slots = [share * pairs * steps // 32 for share in (0, 12, 19, 27)]
     load_x = pltpu.make_async_copy(x_all, x_s, local_sems.at[0])
     load_base = pltpu.make_async_copy(base_all, base_s, local_sems.at[1])
     load_back = pltpu.make_async_copy(gate_back_all, back, local_sems.at[8])
@@ -880,7 +881,7 @@
                 pl.when(slot == at)(functools.partial(first_phase, number))
 
         scan_back_block(
-            coef, pre, step_in, scan_grad, flags, starts, step_w, decay_t, skip,
+            coef, act_in, size_in, step_in, scan_grad, flags, starts, step_w, decay_t, skip,
             act_grads.at[lax.rem(pid, 2)], coef_grads.at[pid], small, scan_spare, between,
         )
         coef_copy(pid).start()
@@ -1090,6 +1091,7 @@
     assert length // CHUNK * states == length
     row_outs = [
         (width, BF16), (width, BF16), (half, F32), (half, F32), (half, F32), None, (half, F32), (half, F32),
+        (half, F32), (half, F32),
         (half, BF16), (half, F32), (width, BF16), (width, BF16),
     ]
     row_f32, row_low = pltpu.VMEM((length, half), F32), pltpu.VMEM((length, half), BF16)
@@ -1100,7 +1102,7 @@
     def pair_of_sems(count):
         return [pltpu.SemaphoreType.DMA((count,)), pltpu.SemaphoreType.DMA((count,))]
 
-    (x, normed_a, conv_in, conv_pre, gate_z, coef, step_pre, scan_out, gated, starts, branch,
+    (x, normed_a, conv_in, conv_pre, gate_z, coef, step_pre, step_size, conv_act, scan_out, gated, starts, branch,
      branch_other) = pl.pallas_call(
         front_kernel,
         in_specs=[pl.BlockSpec(memory_space=pltpu.VMEM)] * 2 + [pl.BlockSpec(memory_space=pl.ANY)]
@@ -1114,7 +1116,7 @@
         scratch_shapes=[
             x_low, x_low, pltpu.VMEM((length + 8, half), F32), row_f32, row_f32,
             pltpu.VMEM(block_coef, F32), pltpu.VMEM(block_coef, F32), pltpu.VMEM(block_coef, F32),
-            row_f32, row_f32, row_low, row_f32, x_low, x_low,
+            row_f32, row_f32, row_f32, row_f32, row_low, row_f32, x_low, x_low,
             [pltpu.VMEM((width, half), BF16), pltpu.VMEM((width, half), BF16)]
             + [pltpu.VMEM((array.shape[0], half), array.dtype)
                for array in (state_t, step_proj, decay_t, skip, taps, conv_b, step_b)]
@@ -1122,7 +1124,7 @@
             [pltpu.VMEM((states, half), F32), block_f32, block_f32, plain_f32,
              pltpu.VMEM((ROWS_STEP, wide), BF16), pltpu.VMEM((STRETCH * wide, half), BF16)],
             pltpu.SemaphoreType.DMA((11,)), pair_of_sems(2), pair_of_sems(blocks), pair_of_sems(blocks),
-            pltpu.SemaphoreType.DMA((9, blocks)), pltpu.SemaphoreType.DMA((3,)),
+            pltpu.SemaphoreType.DMA((11, blocks)), pltpu.SemaphoreType.DMA((3,)),
         ],
         compiler_params=pltpu.CompilerParams(
             vmem_limit_bytes=VMEM_BYTES, collective_id=2, has_side_effects=True
@@ -1189,10 +1191,9 @@
     plan_last, land_last = sum_plan(
         counts, [(0, width // 2, 0), (0, width // 2, 0), (1, 128, 0), (0, 16, -1)]
     )
-    tile_f32 = pltpu.VMEM((half // 128, wide, 128), F32)
-    tile_low = pltpu.VMEM((wide, half), BF16)
-    fold_low = pltpu.VMEM((wide, 128), BF16)
-    chunk_spare = [tile_f32, tile_f32, tile_low, tile_low, fold_low, fold_low]
+    tile_f32 = pltpu.VMEM((2, half // 128, wide, 128), F32)
+    tile_low = pltpu.VMEM((2, wide, half), BF16)
+    own_f32 = pltpu.VMEM((ROWS_STEP, wide), F32)
 
     def now(i):
         return jnp.maximum(steps - 1 - i, 0)
@@ -1207,7 +1208,8 @@
         return (array, array.shape, None)
 
     ins = [
-        (coef, (None, coefs, ROWS_STEP), lambda i: (now(i), 0, 0)), back_rows(conv_pre, now), back_rows(step_pre, now),
+        (coef, (None, coefs, ROWS_STEP), lambda i: (now(i), 0, 0)), back_rows(conv_act, now),
+        back_rows(step_size, now), back_rows(step_pre, now),
         back_rows(scan_grad, now), back_rows(flags, now),
         (starts, (ROWS_STEP // CHUNK * states, half), lambda i: (now(i), 0)),
         back_rows(conv_pre, late_at), back_rows(conv_in, late_at), back_rows(normed_a, late_at),
@@ -1234,7 +1236,7 @@
             pltpu.SemaphoreType.DMA((len(weights_all),)),
             [pltpu.VMEM((states, half), F32), block_f32,
              block_f32, block_f32, block_f32, pltpu.VMEM((ROWS_STEP, wide), BF16), plain_f32,
-             plain_f32, chunk_spare, chunk_spare],
+             plain_f32, own_f32, own_f32, tile_f32, tile_f32, tile_low, tile_low, tile_low],
             pltpu.VMEM((small_rows, half), F32),
             pltpu.VMEM((2, ROWS_STEP, half), F32),
             pltpu.VMEM((steps, coefs, ROWS_STEP), F32),
@@ -1268,25 +1270,26 @@
         ),
         name="back",
     )(*[a for a, _, _ in ins], x, base, gate_back, weights_all)
-    quarter = width // 4
-    eighth = width // 8
+    cuts = 8
+    quarter = width // cuts
+    eighth = width // (2 * cuts)
 
     def from_sum(total, size, first_row):
         return (total, (parts, size, width), lambda i, sel: (0, first_row // size + i, 0))
 
     def out_parts(size):
-        return ((parts, 4 * size, width), F32, (parts, size, width), lambda i, sel: (0, i, 0))
+        return ((parts, cuts * size, width), F32, (parts, size, width), lambda i, sel: (0, i, 0))
 
     results, t_in, t_out, t_query, t_key, t_value, t_mixed, *smalls = call(
-        functools.partial(assemble_kernel, (coefs, rank, states)), sel, 4,
-        [(kept, (piece_len // 4, width), lambda i, sel: (i, 0)),
-         (got, (piece_len // 4, width), lambda i, sel: (i, 0)),
+        functools.partial(assemble_kernel, (coefs, rank, states)), sel, cuts,
+        [(kept, (piece_len // cuts, width), lambda i, sel: (i, 0)),
+         (got, (piece_len // cuts, width), lambda i, sel: (i, 0)),
          from_sum(early, quarter, 0), from_sum(early, eighth, width),
          from_sum(early, eighth, width + width // 2), from_sum(early, quarter, attn_rows),
          from_sum(early, quarter, attn_rows + half), from_sum(late, quarter, 0),
          (late, (parts, 128, width), lambda i, sel: (0, width // 128, 0)),
          (late, (parts, 16, width), lambda i, sel: (0, (width + 128) // 16, 0))],
-        [((1, 2, piece_len, width), F32, (1, 2, piece_len // 4, width), lambda i, sel: (0, 0, i, 0)),
+        [((1, 2, piece_len, width), F32, (1, 2, piece_len // cuts, width), lambda i, sel: (0, 0, i, 0)),
          ((width, 4 * half), F32, (quarter, 4 * half), lambda i, sel: (i, 0)),
          out_parts(quarter), ((width, width), F32, (quarter, width), lambda i, sel: (i, 0)),
          ((width, width), F32, (quarter, width), lambda i, sel: (i, 0)), out_parts(eighth),

time: 181 us -> 180 us (level)
    pallas_call x1, Pallas kernels: 97.8 us -> 95.4 us  [local(): pl.pallas_call(functools.partial(back_kernel, plan, plan_last, steps), gr...]
where the time goes in v3:
time: 180 us
  Pallas kernels  176 us (98%)
  other arithmetic  2.07 us (1%)
    pallas_call x1, Pallas kernels, local(): pl.pallas_call(functools.partial(back_kernel, plan, plan_last, steps), gr...  95.4 us
    pallas_call x1, Pallas kernels, local(): pl.pallas_call(front_kernel, in_specs=[pl.BlockSpec(memory_space=pltpu.VM...  36.2 us
    pallas_call x1, Pallas kernels, local(): pl.pallas_call(middle_kernel, in_specs=[vmem_spec] * 5 + [any_spec] * 5 +...  34 us
    pallas_call x1, Pallas kernels, call(): pl.pallas_call(body, grid_spec=pltpu.PrefetchScalarGridSpec(num_scalar_pr...  10.6 us

profile of v3, /device:TPU:0, one launch (start us, length us, event | category | flops | bytes accessed | tf_op | source)
XLA Modules:
  0.0 179.7 jit_solution(44425551921424436)
XLA Ops:
  0.6 0.0 copy-start
  0.7 0.6 pad_add_fusion.sel
  1.2 0.1 copy-done
  1.4 0.6 convert_reduce_fusion
  1.9 0.0 copy-start.1
  1.9 0.1 fusion.2
  2.1 0.1 stack.32
  2.2 0.3 copy.39
  2.4 0.8 convert_element_type.7.flags.flags_late
  3.3 36.2 %front.1 = (bf16[1024,512]{1,0:T(8,128)(2,1)}, bf16[1024,512]{1,0:T(8,128)(2,1)}, f32[1024,512]{1,0:T(8,128)}, f32[1024,512]{1,0:T(8,128)}, f32[1024,512]{1,0:T(...) custom-call(f32[1024,8]{1,0:T(8,128)} %convert_element_type.7.flags., ...), custom_call_target="tpu_custom_call" | custom-call | flops 16777216000 | bytes 16777216 | tf_op jit(solution)/shard_map/front/pallas_call | solution.py:1106
  39.5 0.0 copy-done.1
  39.5 34.0 %middle.1 = (f32[1024,512]{1,0:T(8,128)}, f32[1024,512]{1,0:T(8,128)}, f32[1024,512]{1,0:T(8,128)}, bf16[2048,512]{1,0:T(8,128)(2,1)}, f32[1,512]{1,0:T(1,128)}) custom-call(bf16[1024,512]{1,0:T(8,128)(2,1)} %get-tuple-element.59.x.x_all, bf16[1024,512]{1,0:T(8,128)(2,1)} %get-tuple-element.60.part_a, bf16[1024,512]{1,0:T(8,128)(2,1)} %get-tuple-element.61.part_b, ...), custom_call_target="tpu_custom_call" | custom-call | flops 10737418240 | bytes 16777216 | tf_op jit(solution)/shard_map/middle/pallas_call | solution.py:1154
  73.5 95.4 %back.1 = (bf16[2,2048,512]{2,1,0:T(8,128)(2,1)}, bf16[2,656,512]{2,1,0:T(8,128)(2,1)}, f32[512,512]{1,0:T(8,128)}, bf16[512,512]{1,0:T(8,128)(2,1)}) custom-call(f32[4,64,256]{2,1,0:T(8,128)} %get-tuple-element.55.coef, f32[1024,512]{1,0:T(8,128)} %get-tuple-element.56.act_in, f32[1024,512]{1,0:T(8,128)} %get-tuple-element.57.size_in, ...), custom_call_target="tpu_custom_call" | custom-call | flops 50331648000 | bytes 33554432 | tf_op jit(solution)/shard_map/back/pallas_call | solution.py:1224
  168.9 10.6 %assemble.1 = (f32[1,2,512,512]{3,2,1,0:T(8,128)}, f32[512,2048]{1,0:T(8,128)}, f32[2,512,512]{2,1,0:T(8,128)}, f32[512,512]{1,0:T(8,128)}, f32[512,512]{1,0:T(8...) custom-call(s32[2]{0:T(128)} %pad_add_fusion.sel, ...), custom_call_target="tpu_custom_call" | custom-call | bytes 26574848 | tf_op jit(solution)/shard_map/assemble/pallas_call | solution.py:90
  (6 shorter events, 0.1 us)
Async XLA Ops:
  0.6 0.7 copy-start
  1.9 37.6 %copy-start.1 = (s32[1024]{0:T(1024)}, s32[1024]{0:T(1024)S(1)}, u32[]{:S(2)}) copy-start(s32[1024]{0:T(1024)S(1)} %convert_reduce_fusion) | copy-start | bytes 12292

commit v4 on v0

--- a/solution.py
+++ b/solution.py
@@ -15,7 +15,7 @@
 STRETCH = 8
 ROWS_STEP = 256
 QUERY_BLOCK = 256
-KEY_TILE = 128
+KEY_TILE = 64
 VMEM_BYTES = 58 * 1024 * 1024
 F32 = jnp.float32
 BF16 = jnp.bfloat16

time: 178 us -> 178 us (level)
  no operation moved by 1% of the time
where the time goes in v4:
time: 178 us; the launch traced here: 177 us
  Pallas kernels  174 us (98%)
  other arithmetic  2.07 us (1%)
    pallas_call x1, Pallas kernels, local(): pl.pallas_call(functools.partial(back_kernel, plan, plan_last, steps), gr...  94.6 us
    pallas_call x1, Pallas kernels, local(): pl.pallas_call(front_kernel, in_specs=[pl.BlockSpec(memory_space=pltpu.VM...  36.2 us
    pallas_call x1, Pallas kernels, local(): pl.pallas_call(middle_kernel, in_specs=[vmem_spec] * 5 + [any_spec] * 5 +...  33.9 us
    pallas_call x1, Pallas kernels, call(): pl.pallas_call(body, grid_spec=pltpu.PrefetchScalarGridSpec(num_scalar_pr...  9.22 us

profile of v4, /device:TPU:0, one launch (start us, length us, event | category | flops | bytes accessed | tf_op | source)
XLA Modules:
  0.0 177.3 jit_solution(9812397921977792570)
XLA Ops:
  0.6 0.0 copy-start
  0.7 0.6 pad_add_fusion.sel
  1.2 0.1 copy-done
  1.4 0.6 convert_reduce_fusion
  1.9 0.0 copy-start.1
  1.9 0.1 fusion.2
  2.1 0.1 stack.32
  2.2 0.3 copy.39
  2.4 0.8 convert_element_type.7.flags.flags_late
  3.3 36.2 %front.1 = (bf16[1024,512]{1,0:T(8,128)(2,1)}, bf16[1024,512]{1,0:T(8,128)(2,1)}, f32[1024,512]{1,0:T(8,128)}, f32[1024,512]{1,0:T(8,128)}, f32[1024,512]{1,0:T(...) custom-call(f32[1024,8]{1,0:T(8,128)} %convert_element_type.7.flags., ...), custom_call_target="tpu_custom_call" | custom-call | flops 16777216000 | bytes 16777216 | tf_op jit(solution)/shard_map/front/pallas_call | solution.py:1097
  39.4 0.0 copy-done.1
  39.5 33.9 %middle.1 = (f32[1024,512]{1,0:T(8,128)}, f32[1024,512]{1,0:T(8,128)}, f32[1024,512]{1,0:T(8,128)}, bf16[2048,512]{1,0:T(8,128)(2,1)}, f32[1,512]{1,0:T(1,128)}) custom-call(bf16[1024,512]{1,0:T(8,128)(2,1)} %get-tuple-element.56.x.x_all, bf16[1024,512]{1,0:T(8,128)(2,1)} %get-tuple-element.57.part_a, bf16[1024,512]{1,0:T(8,128)(2,1)} %get-tuple-element.58.part_b, ...), custom_call_target="tpu_custom_call" | custom-call | flops 10737418240 | bytes 16777216 | tf_op jit(solution)/shard_map/middle/pallas_call | solution.py:1141
  73.3 94.6 %back.1 = (bf16[2,2048,512]{2,1,0:T(8,128)(2,1)}, bf16[2,640,512]{2,1,0:T(8,128)(2,1)}, f32[512,512]{1,0:T(8,128)}, bf16[512,512]{1,0:T(8,128)(2,1)}) custom-call(f32[4,64,256]{2,1,0:T(8,128)} %get-tuple-element.53.coef, f32[1024,512]{1,0:T(8,128)} %get-tuple-element.54.pre.pre_late, f32[1024,512]{1,0:T(8,128)} %get-tuple-element.55.step_in, ...), custom_call_target="tpu_custom_call" | custom-call | flops 50331648000 | bytes 33554432 | tf_op jit(solution)/shard_map/back/pallas_call | solution.py:1211
  167.9 9.2 %assemble.1 = (f32[1,2,512,512]{3,2,1,0:T(8,128)}, f32[512,2048]{1,0:T(8,128)}, f32[2,512,512]{2,1,0:T(8,128)}, f32[512,512]{1,0:T(8,128)}, f32[512,512]{1,0:T(8...) custom-call(s32[2]{0:T(128)} %pad_add_fusion.sel, ...), custom_call_target="tpu_custom_call" | custom-call | bytes 25165824 | tf_op jit(solution)/shard_map/assemble/pallas_call | solution.py:90
  (6 shorter events, 0.1 us)
Async XLA Ops:
  0.6 0.7 copy-start
  1.9 37.5 %copy-start.1 = (s32[1024]{0:T(1024)}, s32[1024]{0:T(1024)S(1)}, u32[]{:S(2)}) copy-start(s32[1024]{0:T(1024)S(1)} %convert_reduce_fusion) | copy-start | bytes 12292
